TPU v7x, 128 devices: a whole 4x4x4 slice. The times are simulated.
128 devices in a mesh: dp: 4 (over z_lo, core), list: 32 (over z_hi, x, y).
Axes of the slice: x: 4, y: 4, z: 4 (z_hi: 2, z_lo: 2; z = z_hi * 2 + z_lo), core: 2. Of those that a mesh axis runs over, the one named last changes fastest.
Arguments:
- passages: bfloat16 [65536, 768], P(('dp', 'list')), may hold values from -8 to 8
- centroids: bfloat16 [8192, 768], P('list'), may hold values from -6 to 6
Outputs:
- new_centroids: float32 [8192, 768], P('list', 'dp')
- list_mass: float32 [8192], P('list')
All inputs are finite; a program needn't handle non-finite values.
Results may differ from a plain program's by a relative error of at most 0.0065.
Values may be sent and summed in bfloat16 or wider, within the bound.
A program may use at most 128 MiB of HBM per device.

v0:
```python
import jax
import jax.numpy as jnp
from jax import lax
from jax.sharding import PartitionSpec as P

ITERS = 3


def unit(values):
    wide = values.astype(jnp.float32)
    return (wide * lax.rsqrt(jnp.sum(wide * wide, axis=-1, keepdims=True) + 1e-06)).astype(
        jnp.bfloat16
    )


def transposed_product(left, right):
    return lax.dot_general(
        left, right, (((0,), (0,)), ((), ())), preferred_element_type=jnp.float32
    )


def on_device(passages, centroids):
    row_unit = unit(passages)
    cent_unit = unit(centroids)
    n_list = lax.axis_size("list")
    n_data = lax.axis_size("dp")
    local_lists = cent_unit.shape[0]
    target = jnp.float32(row_unit.shape[0] * n_list * n_data / (local_lists * n_list))
    group = lax.all_gather(row_unit, "list", axis=0, tiled=True)
    kernel = jnp.exp(20.0 * jnp.dot(group, cent_unit.T, preferred_element_type=jnp.float32))
    row_scale = jnp.ones((group.shape[0],), jnp.float32)
    col_scale = jnp.ones((local_lists,), jnp.float32)
    for step in range(ITERS):
        col_scale = target / lax.psum(jnp.dot(row_scale, kernel), "dp")
        row_scale = 1.0 / lax.psum(jnp.dot(kernel, col_scale), "list")
    plan = kernel * row_scale[:, None] * col_scale[None, :]
    soft_part = transposed_product(plan.astype(jnp.bfloat16), group)
    mass_part = jnp.sum(plan, axis=0)
    width = group.shape[1] // n_data
    soft_all, list_mass = lax.psum((soft_part, mass_part), "dp")
    mine = lax.dynamic_slice_in_dim(soft_all, lax.axis_index("dp") * width, width, 1)
    return (mine / list_mass[:, None], list_mass)


def solution(mesh):
    return jax.shard_map(
        on_device,
        mesh=mesh,
        in_specs=(P(("dp", "list"), None), P("list", None)),
        out_specs=(P("list", "dp"), P("list")),
        check_vma=False,
    )
```

profile of v0, /device:TPU:1, one launch (start us, length us, event | category | flops | bytes accessed | tf_op | source)
XLA Modules:
  0.0 1295.4 jit_solution(13300269440276384895)
XLA Ops:
  7.2 0.0 all-gather.2.cloned.1.call-start
  7.2 1.4 fusion.7
  8.6 2.3 fusion.8
  10.9 0.0 all-reduce.5.cloned.1.call-start
  10.9 1.2 fusion.9
  12.1 210.5 %all-gather.2.cloned.1.call-done = bf16[16384,768]{1,0:T(8,128)(2,1)} async-done(((bf16[512,768]{1,0:T(8,128)(2,1)}), bf16[16384,768]{1,0:T(8,128)(2,1)}) %all-gather.2.cloned.1.call-update) | async-done | bytes 25165840 | tf_op jit(solution)/shard_map/all_gather | solution.py:29
  222.6 15.0 %fusion = f32[16384,256]{1,0:T(8,128)} fusion(bf16[16384,768]{1,0:T(8,128)(2,1)} %all-gather.2.cloned.1.call-done, bf16[256,768]{1,0:T(8,128)(2,1)} %param.3, f32[256]{0:T(256)S(1)} %add_rsqrt_fusion.1), kind=kOutput, calls=%fused_computation.1 | convolution fusion | flops 6447235072 | bytes 42337280 | tf_op jit(solution)/shard_map/dot_general | solution.py:30
  237.7 7.0 fusion.13
  244.6 6.1 psum.56
  250.7 8.7 fusion.16
  259.4 0.0 all-reduce.5.cloned.1.call-update
  259.4 0.0 all-reduce.7.cloned.1.call-start
  259.5 298.8 %all-reduce.5.cloned.1.call-done = f32[16384]{0:T(1024)} async-done(((f32[16384]{0:T(1024)}), f32[16384]{0:T(1024)}) %all-reduce.5.cloned.1.call-update) | async-done | bytes 65552 | tf_op jit(solution)/shard_map/psum | solution.py:35
  558.2 0.9 broadcast_divide_fusion.1
  559.1 7.0 fusion.17
  566.1 15.8 %psum.58 = f32[256]{0:T(256)S(1)} all-reduce(f32[256]{0:T(256)S(1)} %bitcast.31), channel_id=1, replica_groups=mesh['dp'=4,'list'=32] {'dp'}, use_global_device_ids=true, to_apply=%region_4.0 | all-reduce | flops 256 | bytes 2048 | tf_op jit(solution)/shard_map/psum | solution.py:34
  581.9 8.7 fusion.18
  590.6 0.0 all-reduce.7.cloned.1.call-update
  590.6 0.0 all-reduce.9.cloned.1.call-start
  590.7 297.7 %all-reduce.7.cloned.1.call-done = f32[16384]{0:T(1024)} async-done(((f32[16384]{0:T(1024)}), f32[16384]{0:T(1024)}) %all-reduce.7.cloned.1.call-update) | async-done | bytes 65552 | tf_op jit(solution)/shard_map/psum | solution.py:35
  888.4 0.9 broadcast_divide_fusion
  889.2 7.0 fusion.19
  896.2 16.0 %psum.60 = f32[256]{0:T(256)S(1)} all-reduce(f32[256]{0:T(256)S(1)} %bitcast.33), channel_id=1, replica_groups=mesh['dp'=4,'list'=32] {'dp'}, use_global_device_ids=true, to_apply=%region_6.0 | all-reduce | flops 256 | bytes 2048 | tf_op jit(solution)/shard_map/psum | solution.py:34
  912.2 8.7 fusion.20
  920.9 0.0 all-reduce.11.cloned.1.call-start
  921.0 297.7 %all-reduce.9.cloned.1.call-done = f32[16384]{0:T(1024)} async-done(((f32[16384]{0:T(1024)}), f32[16384]{0:T(1024)}) %all-reduce.9.cloned.1.call-update) | async-done | bytes 65552 | tf_op jit(solution)/shard_map/psum | solution.py:35
  1218.7 0.9 broadcast_divide_fusion.2
  1219.5 20.1 %fusion.3 = f32[256,768]{0,1:T(8,128)} fusion(bf16[16384,768]{1,0:T(8,128)(2,1)} %all-gather.2.cloned.1.call-done, f32[16384,256]{1,0:T(8,128)} %fusion, f32[256]{0:T(256)S(1)} %broadcast_divide_fusion.3, f32[16384]{0:T(1024)S(1)} %broadcast_divide_fusion.2), kind=kOutput, calls=%fused_computation.5 | convolution fusion | flops 6455033856 | bytes 42796032 | tf_op jit(solution)/shard_map/dot_general | solution.py:17
  1239.7 7.2 fusion.1
  1246.8 15.9 %psum.63 = f32[256]{0:T(256)S(1)} all-reduce(f32[256]{0:T(256)S(1)} %fusion.1), channel_id=1, replica_groups=mesh['dp'=4,'list'=32] {'dp'}, use_global_device_ids=true, to_apply=%region_10.0 | all-reduce | flops 256 | bytes 2048 | tf_op jit(solution)/shard_map/psum | solution.py:40
  1262.7 24.5 %all-reduce.11.cloned.1.call-done = f32[256,768]{0,1:T(8,128)} async-done(((f32[256,768]{0,1:T(8,128)}), f32[256,768]{0,1:T(8,128)}) %all-reduce.11.cloned.1.call-update) | async-done | bytes 786448 | tf_op jit(solution)/shard_map/psum | solution.py:40
  1287.2 1.6 dynamic-slice_divide_fusion
  (10 shorter events, 0.1 us)
Async XLA Ops:
  7.2 215.5 %all-gather.2.cloned.1.call-start = ((), (), s32[]{:S(2)}) async-start(), calls=%async_computation | async-start | bytes 25952256 | tf_op jit(solution)/shard_map/all_gather | solution.py:29
  10.9 547.4 %all-reduce.5.cloned.1.call-start = ((), (), s32[]{:S(2)}) async-start(), calls=%async_computation.1 | async-start | bytes 131072 | tf_op jit(solution)/shard_map/psum | solution.py:35
  259.4 629.0 %all-reduce.7.cloned.1.call-start = ((), (), s32[]{:S(2)}) async-start(), calls=%async_computation.2 | async-start | bytes 131072 | tf_op jit(solution)/shard_map/psum | solution.py:35
  590.6 628.1 %all-reduce.9.cloned.1.call-start = ((), (), s32[]{:S(2)}) async-start(), calls=%async_computation.3 | async-start | bytes 131072 | tf_op jit(solution)/shard_map/psum | solution.py:35
  920.9 366.3 %all-reduce.11.cloned.1.call-start = ((), (), s32[]{:S(2)}) async-start(), calls=%async_computation.4 | async-start | bytes 1572864 | tf_op jit(solution)/shard_map/psum | solution.py:40
  1262.7 26.1 %copy-start = (f32[256]{0:T(256)}, f32[256]{0:T(256)S(1)}, u32[]{:S(2)}) copy-start(f32[256]{0:T(256)S(1)} %psum.63) | copy-start | bytes 3076
Sparse Core Ops, SparseCore 0:
  11.0 211.5 all-gather.1
  259.5 298.6 all-reduce.4
  590.7 297.6 all-reduce.6
  921.0 297.6 all-reduce.8
  1239.8 47.3 all-reduce.10
where the time goes:
time: 1300 us
  waiting for transfers between devices  1130 us (87%)
  matrix products  82.1 us (6%)
  blocking collectives  53.8 us (4%)
  other arithmetic  16.2 us (1%)
  between operations  13.8 us (1%)
    psum x3, waiting for transfers between devices, on_device(): row_scale = 1.0 / lax.psum(jnp.dot(kernel, col_scale), 'list')  894 us
    all_gather x1, waiting for transfers between devices, on_device(): group = lax.all_gather(row_unit, 'list', axis=0, tiled=True)  211 us
    psum x3, blocking collectives, on_device(): col_scale = target / lax.psum(jnp.dot(row_scale, kernel), 'dp')  37.9 us
    dot_general x3, matrix products, on_device(): row_scale = 1.0 / lax.psum(jnp.dot(kernel, col_scale), 'list')  26 us
  transfers between devices with their start and end apart: 5, of which 5 were waited for; matrix products, arithmetic and copies ran while one was open for 1% of the time, Pallas kernels for 0%

commit v1 on v0

v1 whole, which is shorter than its diff:
```python
import functools

import jax
import jax.numpy as jnp
from jax import lax
from jax.experimental import pallas as pl
from jax.experimental.pallas import tpu as pltpu
from jax.sharding import PartitionSpec as P

MESH = pl.DeviceIdType.MESH
F32 = jnp.float32
BF16 = jnp.bfloat16

ITERS = 3
D = 768
SIDE = 2048
OWN = 512
CHUNK = 128
GROUP = 256
SUB = 64
TILES = SIDE // 128
TARGET = 8.0
LOG2E20 = 20.0 * 1.4426950408889634

STAGES = (
    tuple((d, 0, e) for e in (0, 1) for d in range(4) if (d, e) != (0, 0)),
    tuple((0, d, 0) for d in (1, 2, 3)),
)
WIDEST = max(len(stage) for stage in STAGES)


def unit(values):
    wide = values.astype(F32)
    return (wide * lax.rsqrt(jnp.sum(wide * wide, axis=-1, keepdims=True) + 1e-06)).astype(BF16)


def spread(row):
    return jnp.broadcast_to(row, (128, 128)).T


def body(
    p_ref, cent_ref, out_ref, mass_ref,
    U, Us, C, K, Kb, csum, cb, colbuf, colrecv, rowbuf, rowrecv,
    Sb, Sr, Rl, Own, Tb, Tr, Tl, F4, Fs, Fr, wt, mbuf, mrecv,
    ag_s, ag_r, ps_s, ps_r, pz_s, pz_r, pf_s, pf_r, col_s, col_r, row_s, row_r,
    rs_s, rs_r, fin_s, fin_r, m_s, m_r,
):
    dp = lax.axis_index("dp")
    li = lax.axis_index("list")
    zl, c = dp // 2, dp % 2
    zh, x, y = li // 16, (li // 4) % 4, li % 4

    def dev(zh_, zl_, x_, y_, c_):
        return (zl_ * 2 + c_, zh_ * 16 + x_ * 4 + y_)

    sibling = dev(zh, zl, x, y, 1 - c)
    partner = dev(1 - zh, 1 - zl, x, y, c)
    partner_sibling = dev(1 - zh, 1 - zl, x, y, 1 - c)
    twin = dev(zh, 1 - zl, x, y, c)
    twin_sibling = dev(zh, 1 - zl, x, y, 1 - c)

    def near(dx, dy, dz):
        return dev(zh, (zl + dz) % 2, (x + dx) % 4, (y + dy) % 4, c)

    peers = [sibling, partner, partner_sibling, twin_sibling]
    for stage in STAGES:
        for delta in stage:
            peers.append(near(*delta))

    barrier = pltpu.get_barrier_semaphore()
    for peer in peers:
        pl.semaphore_signal(barrier, inc=1, device_id=peer, device_id_type=MESH)

    def remote(src, dst, send, recv, device):
        return pltpu.make_async_remote_copy(
            src_ref=src, dst_ref=dst, send_sem=send, recv_sem=recv,
            device_id=device, device_id_type=MESH,
        )

    def along(h, phase, step):
        if (h + phase) % 2 == 0:
            return near(step, 0, 0)
        return near(0, step, 0)

    def place(h, phase):
        return (x, y) if (h + phase) % 2 == 0 else (y, x)

    def ag_rows(h, phase, pos, half):
        if phase == 0:
            n = SUB
            at = h * 1024 + place(h, 0)[1] * GROUP + pos * SUB
        else:
            n = GROUP
            at = h * 1024 + pos * GROUP
        return C.at[pl.ds(pl.multiple_of(at + half * (n // 2), n // 2), n // 2), :]

    def ag_copy(h, phase, way, k, block):
        step = 1 if way == 0 else 3
        half = way if k != 1 else 1 - way
        ref = ag_rows(h, phase, block, half)
        return remote(ref, ref, ag_s.at[h, phase, way, k], ag_r.at[h, phase, way, k], along(h, phase, step))

    def ag_start(h, phase):
        me = place(h, phase)[0]
        for k in (0, 1):
            for way in (0, 1):
                ag_copy(h, phase, way, k, me).start()

    def behind(h, phase, way, k):
        me = place(h, phase)[0]
        if k == 2:
            return (me + 2) % 4
        return (me + (3 if way == 0 else 1)) % 4

    def ag_wait(h, phase, k):
        for way in (0, 1):
            ag_copy(h, phase, way, k, behind(h, phase, way, k)).wait_recv()

    def ag_relay(h, phase):
        for way in (0, 1):
            block = behind(h, phase, way, 0)
            ag_copy(h, phase, way, 0, block).wait_recv()
            ag_copy(h, phase, way, 2, block).start()

    def ag_drain(h, phase):
        me = place(h, phase)[0]
        for way in (0, 1):
            ag_copy(h, phase, way, 0, me).wait_send()
            ag_copy(h, phase, way, 1, me).wait_send()
            ag_copy(h, phase, way, 2, behind(h, phase, way, 0)).wait_send()

    for h in (0, 1):
        first, second = place(h, 0)
        at = pl.multiple_of(h * 1024 + second * GROUP + first * SUB, SUB)
        own = cent_ref[pl.ds(pl.multiple_of(c * 128 + h * SUB, SUB), SUB), :]
        C[pl.ds(at, SUB), :] = unit(own)

    pl.semaphore_wait(barrier, len(peers))
    for h in (0, 1):
        ag_start(h, 0)

    slot = zh * 2 + c
    slot_sib = zh * 2 + 1 - c
    slot_par = (1 - zh) * 2 + c
    slot_far = (1 - zh) * 2 + 1 - c

    def rows(which, k):
        return U.at[pl.ds(pl.multiple_of(which * OWN + k * CHUNK, CHUNK), CHUNK), :]

    def p_sib(which, k):
        return remote(rows(which, k), rows(which, k), ps_s.at[k], ps_r.at[k], sibling)

    def p_z(which, k):
        return remote(rows(which, k), rows(which, k), pz_s.at[k], pz_r.at[k], partner)

    def p_fwd(which, k):
        return remote(rows(which, k), rows(which, k), pf_s.at[k], pf_r.at[k], sibling)

    for k in range(OWN // CHUNK):
        U[pl.ds(pl.multiple_of(slot * OWN + k * CHUNK, CHUNK), CHUNK), :] = unit(
            p_ref[pl.ds(k * CHUNK, CHUNK), :]
        )
        p_z(slot, k).start()
        p_sib(slot, k).start()

    csum[...] = jnp.zeros_like(csum)

    def gemm1(g, q):
        at = pl.multiple_of(g * GROUP, GROUP)
        qt = pl.multiple_of(q * OWN, OWN)
        s = lax.dot_general(
            C[pl.ds(at, GROUP), :], U[pl.ds(qt, OWN), :],
            (((1,), (1,)), ((), ())), preferred_element_type=F32,
        )
        e = jnp.exp2(s * LOG2E20)
        K[pl.ds(at, GROUP), pl.ds(qt, OWN)] = e
        Kb[pl.ds(at, GROUP), pl.ds(qt, OWN)] = e.astype(BF16)
        part = e[:, 0:128] + e[:, 128:256] + (e[:, 256:384] + e[:, 384:512])
        csum[pl.ds(at, GROUP), :] += part

    for h in (0, 1):
        ag_relay(h, 0)
    for h in (0, 1):
        ag_wait(h, 0, 1)
        ag_wait(h, 0, 2)
        ag_start(h, 1)

    for k in range(OWN // CHUNK):
        p_sib(slot_sib, k).wait_recv()

    def forward(k):
        p_z(slot_par, k).wait_recv()
        p_fwd(slot_par, k).start()

    @pl.loop(0, 4)
    def _(i):
        h = i // 2
        gemm1(h * 4 + y * (1 - h) + x * h, zh * 2 + i % 2)

    forward(0)
    for h in (0, 1):
        ag_relay(h, 1)
    forward(1)
    for h in (0, 1):
        ag_wait(h, 1, 1)

    @pl.loop(0, 8)
    def _(i):
        h = i // 4
        pos = (y * (1 - h) + x * h + 1 + 2 * ((i // 2) % 2)) % 4
        gemm1(h * 4 + pos, zh * 2 + i % 2)

    forward(2)
    for h in (0, 1):
        ag_wait(h, 1, 2)

    @pl.loop(0, 4)
    def _(i):
        h = i // 2
        pos = (y * (1 - h) + x * h + 2) % 4
        gemm1(h * 4 + pos, zh * 2 + i % 2)

    forward(3)

    @pl.loop(0, 8)
    def _(g):
        gemm1(g, slot_par)

    for k in range(OWN // CHUNK):
        p_fwd(slot_far, k).wait_recv()

    @pl.loop(0, 8)
    def _(g):
        gemm1(g, slot_far)

    def col_pass(r16):
        r = [jnp.broadcast_to(r16[t : t + 1, :], (8, 128)) for t in range(TILES)]

        @pl.loop(0, SIDE // 64)
        def _(i):
            for s in range(8):
                at = pl.multiple_of(i * 64 + s * 8, 8)
                acc = [None] * 4
                for t in range(TILES):
                    term = K[pl.ds(at, 8), t * 128 : (t + 1) * 128] * r[t]
                    acc[t % 4] = term if acc[t % 4] is None else acc[t % 4] + term
                csum[pl.ds(at, 8), :] = (acc[0] + acc[1]) + (acc[2] + acc[3])

    def fold():
        parts = []
        for b in range(TILES):
            block = csum[b * 128 : (b + 1) * 128, :]
            parts.append(jnp.sum(block.T, axis=0, keepdims=True))
        return jnp.concatenate(parts, axis=0)

    def col_copy(it, st, k):
        return remote(
            colbuf.at[it, st], colrecv.at[it, st, k], col_s.at[st, k], col_r.at[it, st, k],
            near(*STAGES[st][k]),
        )

    def col_send(it, st, value):
        colbuf[it, st] = value
        for k in range(len(STAGES[st])):
            col_copy(it, st, k).start()

    def col_take(it, st):
        total = colbuf[it, st]
        for k in range(len(STAGES[st])):
            col_copy(it, st, k).wait_recv()
            total += colrecv[it, st, k]
        for k in range(len(STAGES[st])):
            col_copy(it, st, k).wait_send()
        return total

    def row_pass():
        def step(i, acc):
            acc = list(acc)
            for s in range(4):
                at = pl.multiple_of(i * 32 + s * 8, 8)
                scale = cb[pl.ds(at, 8), :]
                for t in range(TILES):
                    acc[t] += K[pl.ds(at, 8), t * 128 : (t + 1) * 128] * scale
            return tuple(acc)

        zero = tuple(jnp.zeros((8, 128), F32) for _ in range(TILES))
        acc = lax.fori_loop(0, SIDE // 32, step, zero)
        return jnp.concatenate([jnp.sum(a, axis=0, keepdims=True) for a in acc], axis=0)

    row_peers = (sibling, partner, partner_sibling)

    def row_copy(it, k):
        return remote(rowbuf.at[it], rowrecv.at[it, k], row_s.at[k], row_r.at[it, k], row_peers[k])

    def row_sum(it, value):
        rowbuf[it] = value
        for k in range(3):
            row_copy(it, k).start()
        total = value
        for k in range(3):
            row_copy(it, k).wait_recv()
            total += rowrecv[it, k]
        for k in range(3):
            row_copy(it, k).wait_send()
        return total

    r16 = None
    for it in range(ITERS):
        if it > 0:
            col_pass(r16)
        col_send(it, 0, fold())
        col_send(it, 1, col_take(it, 0))
        c16 = TARGET / col_take(it, 1)
        for b in range(TILES):
            cb[b * 128 : (b + 1) * 128, :] = spread(c16[b : b + 1, :])
        r16 = 1.0 / row_sum(it, row_pass())

    col_pass(r16)
    col_send(ITERS, 0, fold())

    for b in range(TILES):
        scale = spread(r16[b : b + 1, :])
        wide = U[b * 128 : (b + 1) * 128, :].astype(F32)
        Us[b * 128 : (b + 1) * 128, :] = (
            wide * jnp.concatenate([scale] * (D // 128), axis=1)
        ).astype(BF16)

    def gemm2(g):
        at = pl.multiple_of(g * GROUP, GROUP)
        return jnp.dot(Kb[pl.ds(at, GROUP), :], Us[...], preferred_element_type=F32)

    def rs_bufs(phase):
        return (Sb, Sr, Rl, GROUP) if phase == 1 else (Tb, Tr, Tl, SUB)

    def rs_copy(h, phase, way, k):
        sb, sr, rl, n = rs_bufs(phase)
        step = 1 if way == 0 else 3
        m = n // 2
        if k == 0:
            src, dst = sb.at[h, 2, pl.ds(way * m, m), :], rl.at[h, way]
        else:
            half = 1 - way if k == 1 else way
            src, dst = sb.at[h, way, pl.ds(half * m, m), :], sr.at[h, way, pl.ds(half * m, m), :]
        return remote(src, dst, rs_s.at[h, phase, way, k], rs_r.at[h, phase, way, k], along(h, phase, step))

    def rs_far(h, phase, value):
        sb = rs_bufs(phase)[0]
        sb[h, 2] = value.astype(BF16)
        for way in (0, 1):
            rs_copy(h, phase, way, 0).start()

    def rs_near(h, phase, way, value):
        sb, sr, rl, n = rs_bufs(phase)
        m = n // 2
        other = 1 - way
        sb[h, way, pl.ds(other * m, m), :] = value[other * m : (other + 1) * m, :].astype(BF16)
        rs_copy(h, phase, way, 1).start()
        rs_copy(h, phase, way, 0).wait_recv()
        sb[h, way, pl.ds(way * m, m), :] = (
            value[way * m : (way + 1) * m, :] + rl[h, way].astype(F32)
        ).astype(BF16)
        rs_copy(h, phase, way, 2).start()

    def rs_take(h, phase, value):
        sr = rs_bufs(phase)[1]
        for way in (0, 1):
            for k in (1, 2):
                rs_copy(h, phase, way, k).wait_recv()
        return value + sr[h, 0].astype(F32) + sr[h, 1].astype(F32)

    def rs_drain(h, phase):
        for way in (0, 1):
            for k in (0, 1, 2):
                rs_copy(h, phase, way, k).wait_send()

    def group(h, step):
        return h * 4 + (place(h, 1)[0] + step) % 4

    for h in (0, 1):
        rs_far(h, 1, gemm2(group(h, 2)))
    col_send(ITERS, 1, col_take(ITERS, 0))
    for way, step in ((0, 1), (1, 3)):
        for h in (0, 1):
            rs_near(h, 1, way, gemm2(group(h, step)))
    for h in (0, 1):
        Own[h] = gemm2(group(h, 0))
    wbuf = mbuf
    colbuf[ITERS, 1] = col_take(ITERS, 1)
    for h in (0, 1):
        first, second = place(h, 0)
        block = h * 8 + second * 2 + first // 2
        wt[...] = spread(colbuf[ITERS, 1, pl.ds(block, 1), :])
        wbuf[pl.ds(h * SUB, SUB), :] = wt[pl.ds(pl.multiple_of((first % 2) * SUB, SUB), SUB), :]
        at = pl.multiple_of(h * 1024 + second * GROUP + first * SUB, SUB)
        wt[pl.ds(0, SUB), :] = cb[pl.ds(at, SUB), :]
        mrecv[0, pl.ds(h * SUB, SUB), :] = wbuf[pl.ds(h * SUB, SUB), :] * wt[pl.ds(0, SUB), :]
    mass = mrecv[0].T[0:8, :]
    mrecv[1, pl.ds(0, 8), :] = mass
    mass_copy = remote(mrecv.at[1, pl.ds(0, 8), :], mrecv.at[1, pl.ds(8, 8), :], m_s.at[0], m_r.at[0], sibling)
    mass_copy.start()

    for h in (0, 1):
        Own[h] = rs_take(h, 1, Own[h])

    def sub(h, step):
        me = place(h, 0)[0]
        return Own[h, pl.ds(pl.multiple_of(((me + step) % 4) * SUB, SUB), SUB), :]

    for h in (0, 1):
        rs_far(h, 0, sub(h, 2))
    for way, step in ((0, 1), (1, 3)):
        for h in (0, 1):
            rs_near(h, 0, way, sub(h, step))
    for h in (0, 1):
        total = rs_take(h, 0, sub(h, 0))
        weight = wbuf[pl.ds(h * SUB, SUB), :]
        total = total * jnp.concatenate([1.0 / weight] * (D // 128), axis=1)
        for k in range(4):
            piece = total[:, k * 192 : (k + 1) * 192]
            F4[k, pl.ds(h * SUB, SUB), :] = piece
            Fs[k, pl.ds(h * SUB, SUB), :] = piece.astype(BF16)

    fin_peers = (
        (twin, (1 - zl) * 2 + c),
        (sibling, zl * 2 + 1 - c),
        (twin_sibling, (1 - zl) * 2 + 1 - c),
    )

    def fin_copy(k):
        return remote(Fs.at[fin_peers[k][1]], Fr.at[k], fin_s.at[k], fin_r.at[k], fin_peers[k][0])

    for k in (2, 0, 1):
        fin_copy(k).start()
    mass_copy.wait_recv()
    mass_ref[pl.ds(c, 1), :] = mrecv[1, pl.ds(0, 1), :]
    mass_ref[pl.ds(1 - c, 1), :] = mrecv[1, pl.ds(8, 1), :]
    fin_copy(0).wait_recv()
    out_ref[pl.ds(pl.multiple_of(c * 128, 128), 128), :] = F4[dp] + Fr[0].astype(F32)
    fin_copy(1).wait_recv()
    fin_copy(2).wait_recv()
    out_ref[pl.ds(pl.multiple_of((1 - c) * 128, 128), 128), :] = Fr[1].astype(F32) + Fr[2].astype(F32)

    for h in (0, 1):
        for phase in (0, 1):
            ag_drain(h, phase)
            rs_drain(h, phase)
    for k in range(OWN // CHUNK):
        p_z(slot, k).wait_send()
        p_sib(slot, k).wait_send()
        p_fwd(slot_par, k).wait_send()
    mass_copy.wait_send()
    for k in range(3):
        fin_copy(k).wait_send()


def on_device(passages, centroids):
    lists = centroids.shape[0]
    width = D // 4
    chunks = OWN // CHUNK
    dma = pltpu.SemaphoreType.DMA
    vm = pltpu.VMEM
    new, mass = pl.pallas_call(
        body,
        out_shape=(
            jax.ShapeDtypeStruct((lists, width), F32),
            jax.ShapeDtypeStruct((2, 128), F32),
        ),
        in_specs=[pl.BlockSpec(memory_space=pltpu.VMEM)] * 2,
        out_specs=(pl.BlockSpec(memory_space=pltpu.VMEM),) * 2,
        scratch_shapes=[
            vm((SIDE, D), BF16),
            vm((SIDE, D), BF16),
            vm((SIDE, D), BF16),
            vm((SIDE, SIDE), F32),
            vm((SIDE, SIDE), BF16),
            vm((SIDE, 128), F32),
            vm((SIDE, 128), F32),
            vm((ITERS + 1, 2, TILES, 128), F32),
            vm((ITERS + 1, 2, WIDEST, TILES, 128), F32),
            vm((ITERS, TILES, 128), F32),
            vm((ITERS, 3, TILES, 128), F32),
            vm((2, 3, GROUP, D), BF16),
            vm((2, 2, GROUP, D), BF16),
            vm((2, 2, GROUP // 2, D), BF16),
            vm((2, GROUP, D), F32),
            vm((2, 3, SUB, D), BF16),
            vm((2, 2, SUB, D), BF16),
            vm((2, 2, SUB // 2, D), BF16),
            vm((4, 128, width), F32),
            vm((4, 128, width), BF16),
            vm((3, 128, width), BF16),
            vm((128, 128), F32),
            vm((128, 128), F32),
            vm((2, 128, 128), F32),
            dma((2, 2, 2, 3)), dma((2, 2, 2, 3)),
            dma((chunks,)), dma((chunks,)),
            dma((chunks,)), dma((chunks,)),
            dma((chunks,)), dma((chunks,)),
            dma((2, WIDEST)), dma((ITERS + 1, 2, WIDEST)),
            dma((3,)), dma((ITERS, 3)),
            dma((2, 2, 2, 3)), dma((2, 2, 2, 3)),
            dma((3,)), dma((3,)),
            dma((1,)), dma((1,)),
        ],
        compiler_params=pltpu.CompilerParams(
            collective_id=0, has_side_effects=True, vmem_limit_bytes=60 * 1024 * 1024
        ),
        cost_estimate=pl.CostEstimate(
            flops=4 * SIDE * SIDE * D, bytes_accessed=2 * 1024 * 1024, transcendentals=SIDE * SIDE
        ),
        name="sinkhorn",
    )(passages, centroids)
    return new, mass.reshape(lists)


def solution(mesh):
    return jax.shard_map(
        on_device,
        mesh=mesh,
        in_specs=(P(("dp", "list"), None), P("list", None)),
        out_specs=(P("list", "dp"), P("list")),
        check_vma=False,
    )
```

time: 1300 us -> 122 us (0.09)
  waiting for transfers between devices: 1130 us -> 0 us
  Pallas kernels: 0 us -> 118 us
  matrix products: 82.1 us -> 0 us
  blocking collectives: 53.8 us -> 0 us
  other arithmetic: 16.2 us -> 0 us
  between operations: 13.8 us -> 0.64 us
    psum x4 -> x0, waiting for transfers between devices: 919 us -> none  [the longest x3 894 us: on_device(): row_scale = 1.0 / lax.psum(jnp.dot(kernel, col_scale), 'list')]
    all_gather x1 -> x0, waiting for transfers between devices: 211 us -> none  [on_device(): group = lax.all_gather(row_unit, 'list', axis=0, tiled=True)]
    pallas_call x0 -> x1, Pallas kernels: none -> 118 us  [on_device(): pl.pallas_call(body, out_shape=(jax.ShapeDtypeStruct((lists, width), F32)...]
    dot_general x8 -> x0, matrix products: 82.1 us -> none  [the longest x3 26 us: on_device(): row_scale = 1.0 / lax.psum(jnp.dot(kernel, col_scale), 'list')]
    psum x4 -> x0, blocking collectives: 53.8 us -> none  [the longest x3 37.9 us: on_device(): col_scale = target / lax.psum(jnp.dot(row_scale, kernel), 'dp')]
  transfers between devices with their start and end apart: 5 -> 0, of which waited for: 5 -> 0; matrix products, arithmetic and copies ran while one was open for 1% -> 0% of each run, Pallas kernels for 0% -> 0%
where the time goes in v1:
time: 122 us; the launch traced here: 121 us
  Pallas kernels  118 us (97%)
  local copies, waits for them, and re-layouts  2.97 us (2%)
    pallas_call x1, Pallas kernels, on_device(): pl.pallas_call(body, out_shape=(jax.ShapeDtypeStruct((lists, width), F32)...  118 us
    unnamed x4, local copies, waits for them, and re-layouts  2.97 us

profile of v1, /device:TPU:1, one launch (start us, length us, event | category | flops | bytes accessed | tf_op | source)
XLA Modules:
  0.0 121.5 jit_solution(10625274737224088220)
XLA Ops:
  0.6 117.9 %sinkhorn.1 = (f32[256,192]{1,0:T(8,128)}, f32[2,128]{1,0:T(2,128)}) custom-call(bf16[512,768]{1,0:T(8,128)(2,1)} %p_ref.1, bf16[256,768]{1,0:T(8,128)(2,1)} %cent_ref.1), custom_call_target="tpu_custom_call" | custom-call | flops 12884901888 | bytes 2097152 | tf_op jit(solution)/shard_map/sinkhorn/pallas_call | solution.py:462
  118.5 1.7 %copy.4 = f32[256,192]{0,1:T(8,128)} copy(f32[256,192]{1,0:T(8,128)} %get-tuple-element.6) | data formatting | bytes 393216
  120.3 0.0 copy-start
  120.3 0.7 copy-done
  120.9 0.6 copy.6
Async XLA Ops:
  120.3 0.7 copy-start

commit v2 on v0

v2 whole, which is shorter than its diff:
```python
import jax
import jax.numpy as jnp
from jax import lax
from jax.experimental import pallas as pl
from jax.experimental.pallas import tpu as pltpu
from jax.sharding import PartitionSpec as P

MESH = pl.DeviceIdType.MESH
F32 = jnp.float32
BF16 = jnp.bfloat16

ITERS = 3
D = 768
SIDE = 2048
OWN = 512
CHUNK = 128
GROUP = 256
SUB = 64
TILES = SIDE // 128
TARGET = 8.0
LOG2E20 = 20.0 * 1.4426950408889634

WIDTH = D // 4
WAVE = D // 2


def far_first():
    deltas = [(a, b, e) for a in range(4) for b in range(4) for e in (0, 1) if (a, b, e) != (0, 0, 0)]
    return tuple(sorted(deltas, key=lambda d: -(min(d[0], 4 - d[0]) + min(d[1], 4 - d[1]) + d[2])))


PEERS = far_first()


def unit(values):
    wide = values.astype(F32)
    return (wide * lax.rsqrt(jnp.sum(wide * wide, axis=-1, keepdims=True) + 1e-06)).astype(BF16)


def spread(row):
    return jnp.broadcast_to(row, (128, 128)).T


def body(
    p_hbm, cent_hbm, out_ref, mass_ref,
    P_in, C_in, U, Us, C, K, Kb, csum, cb, colbuf, colrecv, rowbuf, rowrecv,
    Sb, Sr, Rl, Acc, Own, Tb, Tr, Fs, Fr, wt, wbuf, mbuf,
    in_s, a0_s, a0_r, a1_s, a1_r, ps_s, ps_r, pz_s, pz_r, pf_s, pf_r, col_s, col_r, row_s, row_r,
    rs_s, rs_r, r2_s, r2_r, fin_s, fin_r, m_s, m_r,
):
    dp = lax.axis_index("dp")
    li = lax.axis_index("list")
    zl, c = dp // 2, dp % 2
    zh, x, y = li // 16, (li // 4) % 4, li % 4

    def dev(zh_, zl_, x_, y_, c_):
        return (zl_ * 2 + c_, zh_ * 16 + x_ * 4 + y_)

    sibling = dev(zh, zl, x, y, 1 - c)
    partner = dev(1 - zh, 1 - zl, x, y, c)
    partner_sibling = dev(1 - zh, 1 - zl, x, y, 1 - c)
    twin = dev(zh, 1 - zl, x, y, c)
    twin_sibling = dev(zh, 1 - zl, x, y, 1 - c)

    def near(dx, dy, dz):
        return dev(zh, (zl + dz) % 2, (x + dx) % 4, (y + dy) % 4, c)

    peers = [near(*delta) for delta in PEERS] + [partner_sibling, partner, twin_sibling, sibling]
    barrier = pltpu.get_barrier_semaphore()
    for peer in peers:
        pl.semaphore_signal(barrier, inc=1, device_id=peer, device_id_type=MESH)

    def remote(src, dst, send, recv, device):
        return pltpu.make_async_remote_copy(
            src_ref=src, dst_ref=dst, send_sem=send, recv_sem=recv,
            device_id=device, device_id_type=MESH,
        )

    p_in = pltpu.make_async_copy(p_hbm, P_in, in_s.at[0])
    c_in = pltpu.make_async_copy(cent_hbm.at[pl.ds(pl.multiple_of(c * 128, 128), 128), :], C_in, in_s.at[1])
    p_in.start()
    c_in.start()

    def along(h, phase, step):
        if (h + phase) % 2 == 0:
            return near(step, 0, 0)
        return near(0, step, 0)

    def place(h, phase):
        return (x, y) if (h + phase) % 2 == 0 else (y, x)

    def block(h, a, b, part, parts):
        n = SUB // parts
        at = h * 1024 + b * GROUP + a * SUB + part * n
        return C.at[pl.ds(pl.multiple_of(at, n), n), :]

    def a0_copy(h, d, sent=True):
        a, b = place(h, 0)
        ref = block(h, a if sent else (a + 4 - d) % 4, b, 0, 1)
        return remote(ref, ref, a0_s.at[h, d - 1], a0_r.at[h, d - 1], along(h, 0, d))

    def a1_copy(h, j, way, k, sent=True):
        a, b = place(h, 0)
        back = (3 if way == 0 else 1)
        src = b if sent else (b + back) % 4
        if k == 2:
            src = (b + (back if sent else 2)) % 4
        half = way if k != 1 else 1 - way
        ref = block(h, (a + 4 - j) % 4, src, half, 2)
        return remote(
            ref, ref, a1_s.at[h, j, way, k], a1_r.at[h, j, way, k], along(h, 1, 1 if way == 0 else 3)
        )

    def a1_start(j):
        for k in (0, 1):
            for h in (0, 1):
                for way in (0, 1):
                    a1_copy(h, j, way, k).start()

    def a1_relay(j):
        for h in (0, 1):
            for way in (0, 1):
                a1_copy(h, j, way, 0, False).wait_recv()
                a1_copy(h, j, way, 2).start()

    def a1_wait(j, k):
        for h in (0, 1):
            for way in (0, 1):
                a1_copy(h, j, way, k, False).wait_recv()

    def rows(zh_, k, core):
        return pl.ds(pl.multiple_of(zh_ * 1024 + k * 256 + core * CHUNK, CHUNK), CHUNK)

    chunks = OWN // CHUNK

    def p_copy(zh_, core, k, send, recv, device):
        ref = U.at[rows(zh_, k, core), :]
        return remote(ref, ref, send.at[k], recv.at[k], device)

    def p_z(k, sent=True):
        return p_copy(zh if sent else 1 - zh, c, k, pz_s, pz_r, partner)

    def p_sib(k, sent=True):
        return p_copy(zh, c if sent else 1 - c, k, ps_s, ps_r, sibling)

    def p_fwd(k, sent=True):
        return p_copy(1 - zh, c if sent else 1 - c, k, pf_s, pf_r, sibling)

    def forward(k):
        p_z(k, False).wait_recv()
        p_fwd(k).start()

    p_in.wait()
    for k in range(chunks):
        U[rows(zh, k, c), :] = unit(P_in[pl.ds(k * CHUNK, CHUNK), :])
    c_in.wait()
    for h in (0, 1):
        a, b = place(h, 0)
        at = pl.multiple_of(h * 1024 + b * GROUP + a * SUB, SUB)
        C[pl.ds(at, SUB), :] = unit(C_in[pl.ds(h * SUB, SUB), :])

    pl.semaphore_wait(barrier, len(peers))
    for h in (0, 1):
        for d in (1, 3):
            a0_copy(h, d).start()
    p_z(0).start()
    for h in (0, 1):
        a0_copy(h, 2).start()
    p_sib(0).start()
    a1_start(0)
    for k in range(1, chunks):
        p_z(k).start()
        p_sib(k).start()

    def gemm1(at, m, qt, n, first):
        s = lax.dot_general(
            C[pl.ds(at, m), :], U[pl.ds(qt, n), :],
            (((1,), (1,)), ((), ())), preferred_element_type=F32,
        )
        e = jnp.exp2(s * LOG2E20)
        K[pl.ds(at, m), pl.ds(qt, n)] = e
        Kb[pl.ds(at, m), pl.ds(qt, n)] = e.astype(BF16)
        part = [e[:, t * 128 : (t + 1) * 128] for t in range(n // 128)]
        while len(part) > 1:
            part = [part[t] + part[t + 1] for t in range(0, len(part), 2)]
        csum[pl.ds(at, m), :] = part[0] if first else csum[pl.ds(at, m), :] + part[0]

    own_rows = pl.multiple_of(zh * 1024, 1024)
    far_rows = pl.multiple_of((1 - zh) * 1024, 1024)

    def own_gemm(step):
        @pl.loop(0, 2)
        def _(h):
            pos = (y * (1 - h) + x * h + step) % 4
            gemm1(pl.multiple_of(h * 1024 + pos * GROUP, GROUP), GROUP, own_rows, 1024, True)

    def far_gemm(k):
        gemm1(0, SIDE, pl.multiple_of(far_rows + k * 256, 256), 256, False)

    for d in (1, 3):
        for h in (0, 1):
            a0_copy(h, d, False).wait_recv()
        a1_start(d)
    for h in (0, 1):
        a0_copy(h, 2, False).wait_recv()
    a1_start(2)
    a1_relay(0)
    for k in range(chunks):
        p_sib(k, False).wait_recv()
    own_gemm(0)
    a1_relay(1)
    forward(0)
    a1_relay(3)
    a1_relay(2)
    for j in (0, 1, 3, 2):
        a1_wait(j, 1)
    own_gemm(1)
    forward(1)
    own_gemm(3)
    for j in (0, 1, 3, 2):
        a1_wait(j, 2)
    own_gemm(2)
    p_fwd(0, False).wait_recv()
    far_gemm(0)
    forward(2)
    p_fwd(1, False).wait_recv()
    far_gemm(1)
    p_fwd(2, False).wait_recv()
    far_gemm(2)
    forward(3)
    p_fwd(3, False).wait_recv()
    far_gemm(3)

    def col_pass(r16):
        r = [jnp.broadcast_to(r16[t : t + 1, :], (8, 128)) for t in range(TILES)]

        @pl.loop(0, SIDE // 64)
        def _(i):
            for s in range(8):
                at = pl.multiple_of(i * 64 + s * 8, 8)
                acc = [None] * 4
                for t in range(TILES):
                    term = K[pl.ds(at, 8), t * 128 : (t + 1) * 128] * r[t]
                    acc[t % 4] = term if acc[t % 4] is None else acc[t % 4] + term
                csum[pl.ds(at, 8), :] = (acc[0] + acc[1]) + (acc[2] + acc[3])

    def fold():
        parts = []
        for b in range(TILES):
            square = csum[b * 128 : (b + 1) * 128, :]
            parts.append(jnp.sum(square.T, axis=0, keepdims=True))
        return jnp.concatenate(parts, axis=0)

    def col_send(it, value):
        colbuf[it] = value
        for k, delta in enumerate(PEERS):
            remote(colbuf.at[it], colrecv.at[it, k], col_s.at[it], col_r.at[it], near(*delta)).start()

    def col_all(it):
        return remote(colrecv.at[it], colrecv.at[it], col_s.at[it], col_r.at[it], near(*PEERS[0]))

    def col_take(it):
        col_all(it).wait_recv()
        return jnp.sum(colrecv[it], axis=0) + colbuf[it]

    def row_pass():
        def step(i, acc):
            acc = list(acc)
            for s in range(4):
                at = pl.multiple_of(i * 32 + s * 8, 8)
                scale = cb[pl.ds(at, 8), :]
                for t in range(TILES):
                    acc[t] += K[pl.ds(at, 8), t * 128 : (t + 1) * 128] * scale
            return tuple(acc)

        zero = tuple(jnp.zeros((8, 128), F32) for _ in range(TILES))
        acc = lax.fori_loop(0, SIDE // 32, step, zero)
        return jnp.concatenate([jnp.sum(a, axis=0, keepdims=True) for a in acc], axis=0)

    row_peers = (partner_sibling, partner, sibling)

    def row_copy(it, k):
        return remote(rowbuf.at[it], rowrecv.at[it, k], row_s.at[it, k], row_r.at[it, k], row_peers[k])

    def row_sum(it, value):
        rowbuf[it] = value
        for k in range(3):
            row_copy(it, k).start()
        total = value
        for k in (2, 1, 0):
            row_copy(it, k).wait_recv()
            total += rowrecv[it, k]
        return total

    r16 = None
    for it in range(ITERS):
        if it > 0:
            col_pass(r16)
        col_send(it, fold())
        c16 = TARGET / col_take(it)
        for b in range(TILES):
            cb[b * 128 : (b + 1) * 128, :] = spread(c16[b : b + 1, :])
        r16 = 1.0 / row_sum(it, row_pass())

    for b in range(TILES):
        scale = spread(r16[b : b + 1, :])
        wide = U[b * 128 : (b + 1) * 128, :].astype(F32)
        Us[b * 128 : (b + 1) * 128, :] = (
            wide * jnp.concatenate([scale] * (D // 128), axis=1)
        ).astype(BF16)

    def gemm2(h, step):
        at = pl.multiple_of(h * 1024 + (place(h, 1)[0] + step) % 4 * GROUP, GROUP)
        return jnp.dot(Kb[pl.ds(at, GROUP), :], Us[...], preferred_element_type=F32)

    HALF = GROUP // 2

    def cols(w):
        return slice(w * WAVE, (w + 1) * WAVE)

    def rs_copy(h, w, way, k):
        lanes = pl.ds(w * WAVE, WAVE)
        if k == 0:
            src, dst = Sb.at[h, 2, pl.ds(way * HALF, HALF), lanes], Rl.at[h, way, :, lanes]
        else:
            half = 1 - way if k == 1 else way
            src, dst = (b.at[h, way, pl.ds(half * HALF, HALF), lanes] for b in (Sb, Sr))
        return remote(
            src, dst, rs_s.at[h, w, way, k], rs_r.at[h, w, way, k], along(h, 1, 1 if way == 0 else 3)
        )

    def rs_add(h, w, way):
        half = pl.ds(way * HALF, HALF)
        rs_copy(h, w, way, 0).wait_recv()
        Sb[h, way, half, cols(w)] = (Acc[h, way, :, cols(w)] + Rl[h, way, :, cols(w)].astype(F32)).astype(BF16)
        rs_copy(h, w, way, 2).start()

    for h in (0, 1):
        Sb[h, 2] = gemm2(h, 2).astype(BF16)
        for w in (0, 1):
            for way in (0, 1):
                rs_copy(h, w, way, 0).start()

    col_pass(r16)
    col_send(ITERS, fold())

    for way, step in ((0, 1), (1, 3)):
        for h in (0, 1):
            value = gemm2(h, step)
            other = 1 - way
            Sb[h, way, pl.ds(other * HALF, HALF), :] = value[other * HALF : (other + 1) * HALF, :].astype(BF16)
            Acc[h, way] = value[way * HALF : (way + 1) * HALF, :]
            rs_copy(h, 0, way, 1).start()
            rs_add(h, 0, way)
            rs_copy(h, 1, way, 1).start()
    for h in (0, 1):
        Own[h] = gemm2(h, 0)
    for way in (0, 1):
        for h in (0, 1):
            rs_add(h, 1, way)

    mass16 = col_take(ITERS)
    colbuf[ITERS + 1] = mass16
    for h in (0, 1):
        a, b = place(h, 0)
        mine = pl.ds(h * SUB, SUB)
        wt[...] = spread(colbuf[ITERS + 1, pl.ds(h * 8 + b * 2 + a // 2, 1), :])
        wbuf[mine, :] = wt[pl.ds(pl.multiple_of((a % 2) * SUB, SUB), SUB), :]
        scale = cb[pl.ds(pl.multiple_of(h * 1024 + b * GROUP + a * SUB, SUB), SUB), :]
        wt[mine, :] = wbuf[mine, :] * scale
        if h == 0:
            held = wt[mine, :]
    mass = jnp.concatenate([held, wt[pl.ds(SUB, SUB), :]], axis=0).T[0:8, :]
    mbuf[0] = mass
    mass_copy = remote(mbuf.at[0], mbuf.at[1], m_s.at[0], m_r.at[0], sibling)
    mass_copy.start()

    def r2_copy(h, w, d):
        lanes = pl.ds(w * WAVE, WAVE)
        return remote(
            Tb.at[h, d - 1, :, lanes], Tr.at[h, d - 1, :, lanes],
            r2_s.at[h, w, d - 1], r2_r.at[h, w, d - 1], along(h, 0, d),
        )

    def sub(h, d):
        return pl.ds(pl.multiple_of((place(h, 0)[0] + d) % 4 * SUB, SUB), SUB)

    for w in (0, 1):
        for h in (0, 1):
            for way in (0, 1):
                for k in (1, 2):
                    rs_copy(h, w, way, k).wait_recv()
            Own[h, :, cols(w)] += Sr[h, 0, :, cols(w)].astype(F32) + Sr[h, 1, :, cols(w)].astype(F32)
            for d in (2, 1, 3):
                Tb[h, d - 1, :, cols(w)] = Own[h, sub(h, d), cols(w)].astype(BF16)
                r2_copy(h, w, d).start()

    fin_peers = (
        (twin, (1 - zl) * 2 + c),
        (sibling, zl * 2 + 1 - c),
        (twin_sibling, (1 - zl) * 2 + 1 - c),
    )

    def fin_copy(k):
        return remote(Fs.at[fin_peers[k][1]], Fr.at[k], fin_s.at[k], fin_r.at[k], fin_peers[k][0])

    for w in (0, 1):
        for h in (0, 1):
            total = Own[h, sub(h, 0), cols(w)]
            for d in (2, 1, 3):
                r2_copy(h, w, d).wait_recv()
                total += Tr[h, d - 1, :, cols(w)].astype(F32)
            weight = 1.0 / wbuf[pl.ds(h * SUB, SUB), :]
            total *= jnp.concatenate([weight] * (WAVE // 128), axis=1)
            Own[h, sub(h, 0), cols(w)] = total
            for k in (0, 1):
                Fs[2 * w + k, pl.ds(h * SUB, SUB), :] = total[:, k * WIDTH : (k + 1) * WIDTH].astype(BF16)
    for k in (2, 0, 1):
        fin_copy(k).start()

    mass_copy.wait_recv()
    mass_ref[0:1, :] = mbuf[c, 0:1, :]
    mass_ref[1:2, :] = mbuf[1 - c, 0:1, :]

    def turned(value):
        return jnp.concatenate(
            [value[:, 0:128].T, jnp.concatenate([value[:, 128:192], jnp.zeros((128, 64), F32)], axis=1).T[0:64, :]],
            axis=0,
        )

    mine = jnp.concatenate([Own[h, sub(h, 0), :] for h in (0, 1)], axis=0)
    own_piece = mine[:, 0:WIDTH]
    for k in (1, 2, 3):
        own_piece = jnp.where(dp == k, mine[:, k * WIDTH : (k + 1) * WIDTH], own_piece)
    fin_copy(1).wait_recv()
    fin_copy(0).wait_recv()
    fin_copy(2).wait_recv()
    out_ref[:, pl.ds(pl.multiple_of(c * 128, 128), 128)] = turned(own_piece + Fr[0].astype(F32))
    out_ref[:, pl.ds(pl.multiple_of((1 - c) * 128, 128), 128)] = turned(Fr[1].astype(F32) + Fr[2].astype(F32))

    for h in (0, 1):
        for d in (1, 2, 3):
            a0_copy(h, d).wait_send()
            for w in (0, 1):
                r2_copy(h, w, d).wait_send()
        for way in (0, 1):
            for k in (0, 1, 2):
                for j in range(4):
                    a1_copy(h, j, way, k).wait_send()
                for w in (0, 1):
                    rs_copy(h, w, way, k).wait_send()
    for k in range(chunks):
        p_z(k).wait_send()
        p_sib(k).wait_send()
        p_fwd(k).wait_send()
    for it in range(ITERS + 1):
        col_all(it).wait_send()
    for it in range(ITERS):
        for k in range(3):
            row_copy(it, k).wait_send()
    mass_copy.wait_send()
    for k in range(3):
        fin_copy(k).wait_send()


def on_device(passages, centroids):
    lists = centroids.shape[0]
    chunks = OWN // CHUNK
    dma = pltpu.SemaphoreType.DMA
    vm = pltpu.VMEM
    new, mass = pl.pallas_call(
        body,
        out_shape=(
            jax.ShapeDtypeStruct((WIDTH, lists), F32),
            jax.ShapeDtypeStruct((2, 128), F32),
        ),
        in_specs=[pl.BlockSpec(memory_space=pl.ANY)] * 2,
        out_specs=(pl.BlockSpec(memory_space=pltpu.VMEM),) * 2,
        scratch_shapes=[
            vm((OWN, D), BF16),
            vm((128, D), BF16),
            vm((SIDE, D), BF16),
            vm((SIDE, D), BF16),
            vm((SIDE, D), BF16),
            vm((SIDE, SIDE), F32),
            vm((SIDE, SIDE), BF16),
            vm((SIDE, 128), F32),
            vm((SIDE, 128), F32),
            vm((ITERS + 2, TILES, 128), F32),
            vm((ITERS + 1, len(PEERS), TILES, 128), F32),
            vm((ITERS, TILES, 128), F32),
            vm((ITERS, 3, TILES, 128), F32),
            vm((2, 3, GROUP, D), BF16),
            vm((2, 2, GROUP, D), BF16),
            vm((2, 2, GROUP // 2, D), BF16),
            vm((2, 2, GROUP // 2, D), F32),
            vm((2, GROUP, D), F32),
            vm((2, 3, SUB, D), BF16),
            vm((2, 3, SUB, D), BF16),
            vm((4, 128, WIDTH), BF16),
            vm((3, 128, WIDTH), BF16),
            vm((128, 128), F32),
            vm((128, 128), F32),
            vm((2, 8, 128), F32),
            dma((2,)),
            dma((2, 3)), dma((2, 3)),
            dma((2, 4, 2, 3)), dma((2, 4, 2, 3)),
            dma((chunks,)), dma((chunks,)),
            dma((chunks,)), dma((chunks,)),
            dma((chunks,)), dma((chunks,)),
            dma((ITERS + 1,)), dma((ITERS + 1,)),
            dma((ITERS, 3)), dma((ITERS, 3)),
            dma((2, 2, 2, 3)), dma((2, 2, 2, 3)),
            dma((2, 2, 3)), dma((2, 2, 3)),
            dma((3,)), dma((3,)),
            dma((1,)), dma((1,)),
        ],
        compiler_params=pltpu.CompilerParams(
            collective_id=0, has_side_effects=True, vmem_limit_bytes=60 * 1024 * 1024
        ),
        cost_estimate=pl.CostEstimate(
            flops=4 * SIDE * SIDE * D, bytes_accessed=2 * 1024 * 1024, transcendentals=SIDE * SIDE
        ),
        name="sinkhorn",
    )(passages, centroids)
    return new.T, mass.reshape(lists)


def solution(mesh):
    return jax.shard_map(
        on_device,
        mesh=mesh,
        in_specs=(P(("dp", "list"), None), P("list", None)),
        out_specs=(P("list", "dp"), P("list")),
        check_vma=False,
    )
```

time: 1300 us -> 110 us (0.08)
  waiting for transfers between devices: 1130 us -> 0 us
  Pallas kernels: 0 us -> 107 us
  matrix products: 82.1 us -> 0 us
  blocking collectives: 53.8 us -> 0 us
  other arithmetic: 16.2 us -> 0 us
  between operations: 13.8 us -> 0.65 us
    psum x4 -> x0, waiting for transfers between devices: 919 us -> none  [the longest x3 894 us: on_device(): row_scale = 1.0 / lax.psum(jnp.dot(kernel, col_scale), 'list')]
    all_gather x1 -> x0, waiting for transfers between devices: 211 us -> none  [on_device(): group = lax.all_gather(row_unit, 'list', axis=0, tiled=True)]
    pallas_call x0 -> x1, Pallas kernels: none -> 107 us  [on_device(): pl.pallas_call(body, out_shape=(jax.ShapeDtypeStruct((WIDTH, lists), F32)...]
    dot_general x8 -> x0, matrix products: 82.1 us -> none  [the longest x3 26 us: on_device(): row_scale = 1.0 / lax.psum(jnp.dot(kernel, col_scale), 'list')]
    psum x4 -> x0, blocking collectives: 53.8 us -> none  [the longest x3 37.9 us: on_device(): col_scale = target / lax.psum(jnp.dot(row_scale, kernel), 'dp')]
  transfers between devices with their start and end apart: 5 -> 0, of which waited for: 5 -> 0; matrix products, arithmetic and copies ran while one was open for 1% -> 0% of each run, Pallas kernels for 0% -> 0%
where the time goes in v2:
time: 110 us; the launch traced here: 109 us
  Pallas kernels  107 us (97%)
  local copies, waits for them, and re-layouts  2.18 us (2%)
    pallas_call x1, Pallas kernels, on_device(): pl.pallas_call(body, out_shape=(jax.ShapeDtypeStruct((WIDTH, lists), F32)...  107 us

profile of v2, /device:TPU:1, one launch (start us, length us, event | category | flops | bytes accessed | tf_op | source)
XLA Modules:
  0.0 109.5 jit_solution(7432107905479766764)
XLA Ops:
  0.6 106.7 %sinkhorn.1 = (f32[192,256]{1,0:T(8,128)}, f32[2,128]{1,0:T(2,128)}) custom-call(bf16[512,768]{1,0:T(8,128)(2,1)} %p_hbm.1, bf16[256,768]{1,0:T(8,128)(2,1)} %cent_hbm.1), custom_call_target="tpu_custom_call" | custom-call | flops 12884901888 | bytes 2097152 | tf_op jit(solution)/shard_map/sinkhorn/pallas_call | solution.py:471
  107.3 0.0 copy-start
  107.3 1.6 %copy.6 = f32[256,192]{0,1:T(8,128)} copy(f32[256,192]{0,1:T(8,128)} %bitcast.2) | data formatting | bytes 393216
  108.9 0.0 copy-done
  108.9 0.6 copy.7
Async XLA Ops:
  107.3 1.6 %copy-start = (f32[2,128]{1,0:T(2,128)S(1)}, f32[2,128]{1,0:T(2,128)}, u32[]{:S(2)}) copy-start(f32[2,128]{1,0:T(2,128)} %get-tuple-element.5) | copy-start | bytes 3076

commit v3 on v2

--- a/solution.py
+++ b/solution.py
@@ -46,7 +46,7 @@
     P_in, C_in, U, Us, C, K, Kb, csum, cb, colbuf, colrecv, rowbuf, rowrecv,
     Sb, Sr, Rl, Acc, Own, Tb, Tr, Fs, Fr, wt, wbuf, mbuf,
     in_s, a0_s, a0_r, a1_s, a1_r, ps_s, ps_r, pz_s, pz_r, pf_s, pf_r, col_s, col_r, row_s, row_r,
-    rs_s, rs_r, r2_s, r2_r, fin_s, fin_r, m_s, m_r,
+    rs_s, rs_r, r2_s, r2_r, fin_s, fin_r, m_s, m_r, ready,
 ):
     dp = lax.axis_index("dp")
     li = lax.axis_index("list")
@@ -65,7 +65,8 @@
     def near(dx, dy, dz):
         return dev(zh, (zl + dz) % 2, (x + dx) % 4, (y + dy) % 4, c)
 
-    peers = [near(*delta) for delta in PEERS] + [partner_sibling, partner, twin_sibling, sibling]
+    peers = [near(d, 0, 0) for d in (1, 2, 3)] + [near(0, d, 0) for d in (1, 2, 3)]
+    peers += [partner, twin, sibling]
     barrier = pltpu.get_barrier_semaphore()
     for peer in peers:
         pl.semaphore_signal(barrier, inc=1, device_id=peer, device_id_type=MESH)
@@ -111,11 +112,10 @@
             ref, ref, a1_s.at[h, j, way, k], a1_r.at[h, j, way, k], along(h, 1, 1 if way == 0 else 3)
         )
 
-    def a1_start(j):
-        for k in (0, 1):
-            for h in (0, 1):
-                for way in (0, 1):
-                    a1_copy(h, j, way, k).start()
+    def a1_start(j, k):
+        for h in (0, 1):
+            for way in (0, 1):
+                a1_copy(h, j, way, k).start()
 
     def a1_relay(j):
         for h in (0, 1):
@@ -160,17 +160,17 @@
         C[pl.ds(at, SUB), :] = unit(C_in[pl.ds(h * SUB, SUB), :])
 
     pl.semaphore_wait(barrier, len(peers))
+    p_z(0).start()
     for h in (0, 1):
         for d in (1, 3):
             a0_copy(h, d).start()
-    p_z(0).start()
     for h in (0, 1):
         a0_copy(h, 2).start()
-    p_sib(0).start()
-    a1_start(0)
+    a1_start(0, 0)
+    for k in range(chunks):
+        p_sib(k).start()
     for k in range(1, chunks):
         p_z(k).start()
-        p_sib(k).start()
 
     def gemm1(at, m, qt, n, first):
         s = lax.dot_general(
@@ -188,56 +188,70 @@
     own_rows = pl.multiple_of(zh * 1024, 1024)
     far_rows = pl.multiple_of((1 - zh) * 1024, 1024)
 
-    def own_gemm(step):
-        @pl.loop(0, 2)
-        def _(h):
-            pos = (y * (1 - h) + x * h + step) % 4
-            gemm1(pl.multiple_of(h * 1024 + pos * GROUP, GROUP), GROUP, own_rows, 1024, True)
-
-    def far_gemm(k):
-        gemm1(0, SIDE, pl.multiple_of(far_rows + k * 256, 256), 256, False)
-
-    for d in (1, 3):
+    def group_at(h, step):
+        return pl.multiple_of(h * 1024 + (place(h, 1)[0] + step) % 4 * GROUP, GROUP)
+
+    def own_gemm(steps):
+        for step in steps:
+            for h in (0, 1):
+                gemm1(group_at(h, step), GROUP, own_rows, 1024, True)
+
+    def far_gemm(k, steps):
+        for step in steps:
+            for h in (0, 1):
+                gemm1(group_at(h, step), GROUP, pl.multiple_of(far_rows + k * 256, 256), 256, False)
+
+    def a0_wait(d):
         for h in (0, 1):
             a0_copy(h, d, False).wait_recv()
-        a1_start(d)
-    for h in (0, 1):
-        a0_copy(h, 2, False).wait_recv()
-    a1_start(2)
+
+    a0_wait(1)
+    a1_start(1, 0)
+    a0_wait(3)
+    a1_start(3, 0)
+    a1_start(0, 1)
+    a0_wait(2)
+    a1_start(2, 0)
+    for j in (1, 3, 2):
+        a1_start(j, 1)
     a1_relay(0)
     for k in range(chunks):
         p_sib(k, False).wait_recv()
-    own_gemm(0)
+    own_gemm((0,))
+    forward(0)
     a1_relay(1)
-    forward(0)
     a1_relay(3)
     a1_relay(2)
+    p_fwd(0, False).wait_recv()
+    far_gemm(0, (0,))
+    forward(1)
     for j in (0, 1, 3, 2):
         a1_wait(j, 1)
-    own_gemm(1)
-    forward(1)
-    own_gemm(3)
+    own_gemm((1, 3))
+    far_gemm(0, (1, 3))
+    p_fwd(1, False).wait_recv()
+    far_gemm(1, (0, 1, 3))
+    forward(2)
     for j in (0, 1, 3, 2):
         a1_wait(j, 2)
-    own_gemm(2)
-    p_fwd(0, False).wait_recv()
-    far_gemm(0)
-    forward(2)
-    p_fwd(1, False).wait_recv()
-    far_gemm(1)
+    pl.semaphore_signal(ready, inc=1, device_id=twin, device_id_type=MESH)
+    own_gemm((2,))
+    far_gemm(0, (2,))
+    far_gemm(1, (2,))
     p_fwd(2, False).wait_recv()
-    far_gemm(2)
+    far_gemm(2, (0, 1, 3, 2))
     forward(3)
     p_fwd(3, False).wait_recv()
-    far_gemm(3)
+    far_gemm(3, (0, 1, 3, 2))
+    pl.semaphore_wait(ready, 1)
 
     def col_pass(r16):
         r = [jnp.broadcast_to(r16[t : t + 1, :], (8, 128)) for t in range(TILES)]
 
-        @pl.loop(0, SIDE // 64)
+        @pl.loop(0, SIDE // 128)
         def _(i):
-            for s in range(8):
-                at = pl.multiple_of(i * 64 + s * 8, 8)
+            for s in range(16):
+                at = pl.multiple_of(i * 128 + s * 8, 8)
                 acc = [None] * 4
                 for t in range(TILES):
                     term = K[pl.ds(at, 8), t * 128 : (t + 1) * 128] * r[t]
@@ -266,15 +280,15 @@
     def row_pass():
         def step(i, acc):
             acc = list(acc)
-            for s in range(4):
-                at = pl.multiple_of(i * 32 + s * 8, 8)
+            for s in range(8):
+                at = pl.multiple_of(i * 64 + s * 8, 8)
                 scale = cb[pl.ds(at, 8), :]
                 for t in range(TILES):
                     acc[t] += K[pl.ds(at, 8), t * 128 : (t + 1) * 128] * scale
             return tuple(acc)
 
         zero = tuple(jnp.zeros((8, 128), F32) for _ in range(TILES))
-        acc = lax.fori_loop(0, SIDE // 32, step, zero)
+        acc = lax.fori_loop(0, SIDE // 64, step, zero)
         return jnp.concatenate([jnp.sum(a, axis=0, keepdims=True) for a in acc], axis=0)
 
     row_peers = (partner_sibling, partner, sibling)
@@ -310,8 +324,7 @@
         ).astype(BF16)
 
     def gemm2(h, step):
-        at = pl.multiple_of(h * 1024 + (place(h, 1)[0] + step) % 4 * GROUP, GROUP)
-        return jnp.dot(Kb[pl.ds(at, GROUP), :], Us[...], preferred_element_type=F32)
+        return jnp.dot(Kb[pl.ds(group_at(h, step), GROUP), :], Us[...], preferred_element_type=F32)
 
     HALF = GROUP // 2
 
@@ -341,23 +354,24 @@
             for way in (0, 1):
                 rs_copy(h, w, way, 0).start()
 
-    col_pass(r16)
-    col_send(ITERS, fold())
-
     for way, step in ((0, 1), (1, 3)):
         for h in (0, 1):
             value = gemm2(h, step)
             other = 1 - way
             Sb[h, way, pl.ds(other * HALF, HALF), :] = value[other * HALF : (other + 1) * HALF, :].astype(BF16)
             Acc[h, way] = value[way * HALF : (way + 1) * HALF, :]
-            rs_copy(h, 0, way, 1).start()
+            for w in (0, 1):
+                rs_copy(h, w, way, 1).start()
+    for way in (0, 1):
+        for h in (0, 1):
             rs_add(h, 0, way)
-            rs_copy(h, 1, way, 1).start()
     for h in (0, 1):
         Own[h] = gemm2(h, 0)
     for way in (0, 1):
         for h in (0, 1):
             rs_add(h, 1, way)
+    col_pass(r16)
+    col_send(ITERS, fold())
 
     mass16 = col_take(ITERS)
     colbuf[ITERS + 1] = mass16
@@ -514,6 +528,7 @@
             dma((2, 2, 3)), dma((2, 2, 3)),
             dma((3,)), dma((3,)),
             dma((1,)), dma((1,)),
+            pltpu.SemaphoreType.REGULAR,
         ],
         compiler_params=pltpu.CompilerParams(
             collective_id=0, has_side_effects=True, vmem_limit_bytes=60 * 1024 * 1024

time: 110 us -> 106 us (0.964)
  Pallas kernels: 107 us -> 103 us
    pallas_call x1, Pallas kernels: 107 us -> 103 us  [on_device(): pl.pallas_call(body, out_shape=(jax.ShapeDtypeStruct((WIDTH, lists), F32)...]
where the time goes in v3:
time: 106 us
  Pallas kernels  103 us (97%)
  local copies, waits for them, and re-layouts  2.18 us (2%)
    pallas_call x1, Pallas kernels, on_device(): pl.pallas_call(body, out_shape=(jax.ShapeDtypeStruct((WIDTH, lists), F32)...  103 us
    unnamed x4, local copies, waits for them, and re-layouts  2.18 us

profile of v3, /device:TPU:1, one launch (start us, length us, event | category | flops | bytes accessed | tf_op | source)
XLA Modules:
  0.0 106.1 jit_solution(5704684830463950604)
XLA Ops:
  0.6 103.3 %sinkhorn.1 = (f32[192,256]{1,0:T(8,128)}, f32[2,128]{1,0:T(2,128)}) custom-call(bf16[512,768]{1,0:T(8,128)(2,1)} %p_hbm.1, bf16[256,768]{1,0:T(8,128)(2,1)} %cent_hbm.1), custom_call_target="tpu_custom_call" | custom-call | flops 12884901888 | bytes 2097152 | tf_op jit(solution)/shard_map/sinkhorn/pallas_call | solution.py:485
  103.9 0.0 copy-start
  103.9 1.6 %copy.6 = f32[256,192]{0,1:T(8,128)} copy(f32[256,192]{0,1:T(8,128)} %bitcast.2) | data formatting | bytes 393216
  105.5 0.0 copy-done
  105.5 0.6 copy.7
Async XLA Ops:
  103.9 1.6 %copy-start = (f32[2,128]{1,0:T(2,128)S(1)}, f32[2,128]{1,0:T(2,128)}, u32[]{:S(2)}) copy-start(f32[2,128]{1,0:T(2,128)} %get-tuple-element.5) | copy-start | bytes 3076

commit v4 on v3

v4 whole, which is shorter than its diff:
```python
import jax
import jax.numpy as jnp
from jax import lax
from jax.experimental import pallas as pl
from jax.experimental.pallas import tpu as pltpu
from jax.sharding import PartitionSpec as P

MESH = pl.DeviceIdType.MESH
F32 = jnp.float32
BF16 = jnp.bfloat16

ITERS = 3
D = 768
LISTS = 1024
ROWS = 4096
OWN = 512
CHUNK = 128
GROUP = 128
SUB = 32
HALFLISTS = LISTS // 2
MINE = 2 * SUB
LT = LISTS // 128
RT = ROWS // 128
TARGET = 8.0
LOG2E20 = 20.0 * 1.4426950408889634

WIDTH = D // 4
WAVE = D // 2


def far_first():
    deltas = [(a, b) for a in range(4) for b in range(4) if (a, b) != (0, 0)]
    return tuple(sorted(deltas, key=lambda d: -(min(d[0], 4 - d[0]) + min(d[1], 4 - d[1]))))


PEERS = far_first()


def unit(values):
    wide = values.astype(F32)
    return (wide * lax.rsqrt(jnp.sum(wide * wide, axis=-1, keepdims=True) + 1e-06)).astype(BF16)


def spread(row):
    return jnp.broadcast_to(row, (128, 128)).T


def body(
    p_hbm, cent_hbm, out_ref, mass_ref,
    P_in, C_in, U, Us, C, K, Kb, csum, cb, colbuf, colrecv, rowbuf, rowrecv,
    Sb, Sr, Rl, Acc, Own, Tb, Tr, Fs, Fr, wt, wbuf, mbuf,
    in_s, a0_s, a0_r, a1_s, a1_r, ps_s, ps_r, pz_s, pz_r, pr_s, pr_r, pf_s, pf_r, col_s, col_r, row_s, row_r,
    rs_s, rs_r, r2_s, r2_r, fin_s, fin_r, m_s, m_r,
):
    dp = lax.axis_index("dp")
    li = lax.axis_index("list")
    zl, c = dp // 2, dp % 2
    zh, x, y = li // 16, (li // 4) % 4, li % 4

    def dev(zh_, zl_, x_, y_, c_):
        return (zl_ * 2 + c_, zh_ * 16 + x_ * 4 + y_)

    z = zh * 2 + zl
    sibling = dev(zh, zl, x, y, 1 - c)

    def up(d, core):
        to = (z + d) % 4
        return dev(to // 2, to % 2, x, y, core)

    def near(dx, dy):
        return dev(zh, zl, (x + dx) % 4, (y + dy) % 4, c)

    peers = [near(d, 0) for d in (1, 2, 3)] + [near(0, d) for d in (1, 2, 3)]
    peers += [up(1, c), up(3, c), sibling]
    barrier = pltpu.get_barrier_semaphore()
    for peer in peers:
        pl.semaphore_signal(barrier, inc=1, device_id=peer, device_id_type=MESH)

    def remote(src, dst, send, recv, device):
        return pltpu.make_async_remote_copy(
            src_ref=src, dst_ref=dst, send_sem=send, recv_sem=recv,
            device_id=device, device_id_type=MESH,
        )

    p_in = pltpu.make_async_copy(p_hbm, P_in, in_s.at[0])
    c_in = pltpu.make_async_copy(cent_hbm.at[pl.ds(pl.multiple_of(dp * MINE, MINE), MINE), :], C_in, in_s.at[1])
    p_in.start()
    c_in.start()

    def along(h, phase, step):
        if (h + phase) % 2 == 0:
            return near(step, 0)
        return near(0, step)

    def place(h, phase):
        return (x, y) if (h + phase) % 2 == 0 else (y, x)

    def block(h, a, b, part, parts):
        n = SUB // parts
        at = h * HALFLISTS + b * GROUP + a * SUB + part * n
        return C.at[pl.ds(pl.multiple_of(at, n), n), :]

    def a0_copy(h, d, sent=True):
        a, b = place(h, 0)
        ref = block(h, a if sent else (a + 4 - d) % 4, b, 0, 1)
        return remote(ref, ref, a0_s.at[h, d - 1], a0_r.at[h, d - 1], along(h, 0, d))

    def a1_copy(h, j, way, k, sent=True):
        a, b = place(h, 0)
        back = (3 if way == 0 else 1)
        src = b if sent else (b + back) % 4
        if k == 2:
            src = (b + (back if sent else 2)) % 4
        half = way if k != 1 else 1 - way
        ref = block(h, (a + 4 - j) % 4, src, half, 2)
        return remote(
            ref, ref, a1_s.at[h, j, way, k], a1_r.at[h, j, way, k], along(h, 1, 1 if way == 0 else 3)
        )

    def a1_start(j, k):
        for h in (0, 1):
            for way in (0, 1):
                a1_copy(h, j, way, k).start()

    def a1_relay(j):
        for h in (0, 1):
            for way in (0, 1):
                a1_copy(h, j, way, 0, False).wait_recv()
                a1_copy(h, j, way, 2).start()

    def a1_wait(j, k):
        for h in (0, 1):
            for way in (0, 1):
                a1_copy(h, j, way, k, False).wait_recv()

    def rows(at, k, core):
        return pl.ds(pl.multiple_of(at * 1024 + k * 256 + core * CHUNK, CHUNK), CHUNK)

    chunks = OWN // CHUNK

    def p_copy(d, core, k, send, recv, device):
        ref = U.at[rows((z + d) % 4, k, core), :]
        return remote(ref, ref, send, recv, device)

    def p_sib(k, sent=True):
        return p_copy(0, c if sent else 1 - c, k, ps_s.at[k], ps_r.at[k], sibling)

    def p_z(k, way, sent=True):
        step = 1 if way == 0 else 3
        return p_copy(0 if sent else 4 - step, c, k, pz_s.at[way, k], pz_r.at[way, k], up(step, c))

    def p_relay(k, sent=True):
        step = 1 if k < 2 else 3
        return p_copy(4 - step if sent else 2, c, k, pr_s.at[k], pr_r.at[k], up(step, c))

    def p_fwd(d, k, sent=True):
        return p_copy(d, c if sent else 1 - c, k, pf_s.at[d - 1, k], pf_r.at[d - 1, k], sibling)

    def p_near(k):
        for way in (0, 1):
            p_z(k, way, False).wait_recv()
            if (k < 2) == (way == 0):
                p_relay(k).start()
        for d in (1, 3):
            p_fwd(d, k).start()

    def p_far(k):
        p_relay(k, False).wait_recv()
        p_fwd(2, k).start()

    p_in.wait()
    for k in range(chunks):
        U[rows(z, k, c), :] = unit(P_in[pl.ds(k * CHUNK, CHUNK), :])
    c_in.wait()
    for h in (0, 1):
        a, b = place(h, 0)
        at = pl.multiple_of(h * HALFLISTS + b * GROUP + a * SUB, SUB)
        C[pl.ds(at, SUB), :] = unit(C_in[pl.ds(h * SUB, SUB), :])

    pl.semaphore_wait(barrier, len(peers))
    for k in (0, 2):
        for way in (0, 1):
            p_z(k, way).start()
    for h in (0, 1):
        for d in (1, 3):
            a0_copy(h, d).start()
    for h in (0, 1):
        a0_copy(h, 2).start()
    a1_start(0, 0)
    for k in range(chunks):
        p_sib(k).start()
    for k in (1, 3):
        for way in (0, 1):
            p_z(k, way).start()

    def gemm1(at, m, qt, n, first):
        s = lax.dot_general(
            C[pl.ds(at, m), :], U[pl.ds(qt, n), :],
            (((1,), (1,)), ((), ())), preferred_element_type=F32,
        )
        e = jnp.exp2(s * LOG2E20)
        K[pl.ds(at, m), pl.ds(qt, n)] = e
        Kb[pl.ds(at, m), pl.ds(qt, n)] = e.astype(BF16)
        part = [e[:, t * 128 : (t + 1) * 128] for t in range(n // 128)]
        while len(part) > 1:
            part = [part[t] + part[t + 1] for t in range(0, len(part), 2)]
        csum[pl.ds(at, m), :] = part[0] if first else csum[pl.ds(at, m), :] + part[0]

    def group_at(h, step):
        return pl.multiple_of(h * HALFLISTS + (place(h, 1)[0] + step) % 4 * GROUP, GROUP)

    def own_gemm(steps):
        for step in steps:
            for h in (0, 1):
                gemm1(group_at(h, step), GROUP, pl.multiple_of(z * 1024, 1024), 1024, True)

    def far_gemm(d, k):
        at = pl.multiple_of((z + d) % 4 * 1024 + k * 256, 256)
        for g in range(0, LISTS, 256):
            gemm1(g, 256, at, 256, False)

    def a0_wait(d):
        for h in (0, 1):
            a0_copy(h, d, False).wait_recv()

    a0_wait(1)
    a1_start(1, 0)
    a0_wait(3)
    a1_start(3, 0)
    a1_start(0, 1)
    a0_wait(2)
    a1_start(2, 0)
    for j in (1, 3, 2):
        a1_start(j, 1)
    a1_relay(0)
    for k in range(chunks):
        p_sib(k, False).wait_recv()
    own_gemm((0,))
    a1_relay(1)
    a1_relay(3)
    p_near(0)
    a1_relay(2)
    for j in (0, 1, 3, 2):
        a1_wait(j, 1)
    own_gemm((1, 3))
    p_near(2)
    for j in (0, 1, 3, 2):
        a1_wait(j, 2)
    own_gemm((2,))
    p_near(1)

    def far_both(k):
        for d in (1, 3):
            p_fwd(d, k, False).wait_recv()
        for d in (1, 3):
            far_gemm(d, k)

    def far_two(k):
        p_fwd(2, k, False).wait_recv()
        far_gemm(2, k)

    far_both(0)
    p_far(0)
    far_both(2)
    p_near(3)
    p_far(2)
    far_both(1)
    far_two(0)
    p_far(1)
    far_two(2)
    far_both(3)
    p_far(3)
    far_two(1)
    far_two(3)

    def col_pass(r16, out):
        strips = 32

        @pl.loop(0, LISTS // (8 * strips))
        def _(i):
            acc = [None] * strips
            for t in range(RT):
                r = jnp.broadcast_to(r16[t : t + 1, :], (8, 128))
                for s in range(strips):
                    at = pl.multiple_of(i * (8 * strips) + s * 8, 8)
                    term = K[pl.ds(at, 8), t * 128 : (t + 1) * 128] * r
                    acc[s] = term if acc[s] is None else acc[s] + term
            for s in range(strips):
                csum[pl.ds(pl.multiple_of(i * (8 * strips) + s * 8, 8), 8), :] = acc[s]

        fold(out)

    def fold(out):
        parts = []
        for b in range(LT):
            square = csum[b * 128 : (b + 1) * 128, :]
            parts.append(jnp.sum(square.T, axis=0, keepdims=True))
        out[...] = jnp.concatenate(parts, axis=0)

    def col_send(it):
        for k, delta in enumerate(PEERS):
            remote(colbuf.at[it], colrecv.at[it, k], col_s.at[it], col_r.at[it], near(*delta)).start()

    def col_all(it):
        return remote(colrecv.at[it], colrecv.at[it], col_s.at[it], col_r.at[it], near(*PEERS[0]))

    def col_take(it):
        col_all(it).wait_recv()
        return jnp.sum(colrecv[it], axis=0) + colbuf[it]

    def row_pass(c16):
        for b in range(LT):
            cb[b * 128 : (b + 1) * 128, :] = spread(c16[b : b + 1, :])

        def step(i, acc):
            acc = list(acc)
            for s in range(8):
                at = pl.multiple_of(i * 64 + s * 8, 8)
                scale = cb[pl.ds(at, 8), :]
                for t in range(RT):
                    acc[t] += K[pl.ds(at, 8), t * 128 : (t + 1) * 128] * scale
            return tuple(acc)

        zero = tuple(jnp.zeros((8, 128), F32) for _ in range(RT))
        acc = lax.fori_loop(0, LISTS // 64, step, zero)
        return jnp.concatenate([jnp.sum(a, axis=0, keepdims=True) for a in acc], axis=0)

    row_peers = [up(2, 1 - c), up(2, c)] + [up(d, 1 - c) for d in (1, 3)] + [up(d, c) for d in (1, 3)] + [sibling]

    def row_send(it, value):
        rowbuf[it] = value
        for k, peer in enumerate(row_peers):
            remote(rowbuf.at[it], rowrecv.at[it, k], row_s.at[it], row_r.at[it], peer).start()

    def row_all(it):
        return remote(rowrecv.at[it], rowrecv.at[it], row_s.at[it], row_r.at[it], sibling)

    def row_sum(it, value):
        row_send(it, value)
        row_all(it).wait_recv()
        return jnp.sum(rowrecv[it], axis=0) + value

    r16 = None
    for it in range(ITERS):
        if it == 0:
            fold(colbuf.at[0])
        else:
            col_pass(r16, colbuf.at[it])
        col_send(it)
        r16 = 1.0 / row_sum(it, row_pass(TARGET / col_take(it)))

    def scale_rows(first, count):
        for b in range(first, first + count):
            scale = spread(r16[b : b + 1, :])
            wide = U[b * 128 : (b + 1) * 128, :].astype(F32)
            Us[b * 128 : (b + 1) * 128, :] = (
                wide * jnp.concatenate([scale] * (D // 128), axis=1)
            ).astype(BF16)

    def gemm2(h, step):
        return jnp.dot(Kb[pl.ds(group_at(h, step), GROUP), :], Us[...], preferred_element_type=F32)

    def gemm2_first(h, step, parts=8):
        total = None
        n = ROWS // parts
        for q in range(parts):
            scale_rows(q * (RT // parts), RT // parts)
            part = jnp.dot(
                Kb[pl.ds(group_at(h, step), GROUP), q * n : (q + 1) * n], Us[q * n : (q + 1) * n, :],
                preferred_element_type=F32,
            )
            total = part if total is None else total + part
        return total

    HALF = GROUP // 2

    def cols(w):
        return slice(w * WAVE, (w + 1) * WAVE)

    def rs_copy(h, w, way, k):
        lanes = pl.ds(w * WAVE, WAVE)
        if k == 0:
            src, dst = Sb.at[h, 2, pl.ds(way * HALF, HALF), lanes], Rl.at[h, way, :, lanes]
        else:
            half = 1 - way if k == 1 else way
            src, dst = (b.at[h, way, pl.ds(half * HALF, HALF), lanes] for b in (Sb, Sr))
        return remote(
            src, dst, rs_s.at[h, w, way, k], rs_r.at[h, w, way, k], along(h, 1, 1 if way == 0 else 3)
        )

    def rs_add(h, w, way):
        half = pl.ds(way * HALF, HALF)
        rs_copy(h, w, way, 0).wait_recv()
        Sb[h, way, half, cols(w)] = (Acc[h, way, :, cols(w)] + Rl[h, way, :, cols(w)].astype(F32)).astype(BF16)
        rs_copy(h, w, way, 2).start()

    for h in (0, 1):
        Sb[h, 2] = (gemm2_first if h == 0 else gemm2)(h, 2).astype(BF16)
        for w in (0, 1):
            for way in (0, 1):
                rs_copy(h, w, way, 0).start()

    for way, step in ((0, 1), (1, 3)):
        for h in (0, 1):
            value = gemm2(h, step)
            other = 1 - way
            Sb[h, way, pl.ds(other * HALF, HALF), :] = value[other * HALF : (other + 1) * HALF, :].astype(BF16)
            Acc[h, way] = value[way * HALF : (way + 1) * HALF, :]
            rs_copy(h, 0, way, 1).start()
    for way in (0, 1):
        for h in (0, 1):
            rs_add(h, 0, way)
            rs_copy(h, 1, way, 1).start()
    for h in (0, 1):
        Own[h] = gemm2(h, 0)
    for way in (0, 1):
        for h in (0, 1):
            rs_add(h, 1, way)
    col_pass(r16, colbuf.at[ITERS])
    col_send(ITERS)

    colbuf[ITERS + 1] = col_take(ITERS)
    held = []
    for h in (0, 1):
        a, b = place(h, 0)
        wt[...] = spread(colbuf[ITERS + 1, pl.ds(h * 4 + b, 1), :])
        wbuf[pl.ds(h * SUB, SUB), :] = wt[pl.ds(pl.multiple_of(a * SUB, SUB), SUB), :]
        scale = cb[pl.ds(pl.multiple_of(h * HALFLISTS + b * GROUP + a * SUB, SUB), SUB), :]
        held.append(wbuf[pl.ds(h * SUB, SUB), :] * scale)
    mass = jnp.concatenate(held + [jnp.zeros((128 - MINE, 128), F32)], axis=0).T[0:8, :]
    mbuf[dp] = mass
    fin_peers = (
        (dev(zh, 1 - zl, x, y, 1 - c), (1 - zl) * 2 + 1 - c),
        (dev(zh, 1 - zl, x, y, c), (1 - zl) * 2 + c),
        (sibling, zl * 2 + 1 - c),
    )

    def mass_copy(k, sent=True):
        slot = mbuf.at[dp if sent else fin_peers[k][1]]
        return remote(slot, slot, m_s.at[k], m_r.at[k], fin_peers[k][0])

    for k in range(3):
        mass_copy(k).start()

    def r2_copy(h, w, d):
        lanes = pl.ds(w * WAVE, WAVE)
        return remote(
            Tb.at[h, d - 1, :, lanes], Tr.at[h, d - 1, :, lanes],
            r2_s.at[h, w, d - 1], r2_r.at[h, w, d - 1], along(h, 0, d),
        )

    def sub(h, d):
        return pl.ds(pl.multiple_of((place(h, 0)[0] + d) % 4 * SUB, SUB), SUB)

    for w in (0, 1):
        for h in (0, 1):
            for way in (0, 1):
                for k in (1, 2):
                    rs_copy(h, w, way, k).wait_recv()
            Own[h, :, cols(w)] += Sr[h, 0, :, cols(w)].astype(F32) + Sr[h, 1, :, cols(w)].astype(F32)
            for d in (2, 1, 3):
                Tb[h, d - 1, :, cols(w)] = Own[h, sub(h, d), cols(w)].astype(BF16)
                r2_copy(h, w, d).start()

    def fin_copy(k, sent=True):
        to = fin_peers[k][1]
        return remote(Fs.at[to if sent else dp], Fr.at[dp if sent else to], fin_s.at[k], fin_r.at[k], fin_peers[k][0])

    for w in (0, 1):
        for h in (0, 1):
            total = Own[h, sub(h, 0), cols(w)]
            for d in (2, 1, 3):
                r2_copy(h, w, d).wait_recv()
                total += Tr[h, d - 1, :, cols(w)].astype(F32)
            weight = 1.0 / wbuf[pl.ds(h * SUB, SUB), :]
            total *= jnp.concatenate([weight] * (WAVE // 128), axis=1)
            for k in (0, 1):
                Fs[2 * w + k, pl.ds(h * SUB, SUB), :] = total[:, k * WIDTH : (k + 1) * WIDTH].astype(Fs.dtype)
    for k in range(3):
        fin_copy(k).start()

    for k in range(3):
        mass_copy(k, False).wait_recv()
    for k in (0, 1):
        mass_ref[k : k + 1, :] = jnp.concatenate([mbuf[2 * k, 0:1, 0:MINE], mbuf[2 * k + 1, 0:1, 0:MINE]], axis=1)

    Fr[dp] = Fs[dp]
    for k in (2, 1, 0):
        fin_copy(k, False).wait_recv()
    for k in (0, 1):
        value = jnp.concatenate([Fr[2 * k], Fr[2 * k + 1]], axis=0).astype(F32)
        out_ref[0:128, k * 128 : (k + 1) * 128] = value[:, 0:128].T
        side = jnp.concatenate([value[:, 128:192], jnp.zeros((128, 64), F32)], axis=1)
        out_ref[128:192, k * 128 : (k + 1) * 128] = side.T[0:64, :]

    for h in (0, 1):
        for d in (1, 2, 3):
            a0_copy(h, d).wait_send()
            for w in (0, 1):
                r2_copy(h, w, d).wait_send()
        for way in (0, 1):
            for k in (0, 1, 2):
                for j in range(4):
                    a1_copy(h, j, way, k).wait_send()
                for w in (0, 1):
                    rs_copy(h, w, way, k).wait_send()
    for k in range(chunks):
        for way in (0, 1):
            p_z(k, way).wait_send()
        p_sib(k).wait_send()
        p_relay(k).wait_send()
        for d in (1, 2, 3):
            p_fwd(d, k).wait_send()
    for it in range(ITERS + 1):
        col_all(it).wait_send()
    for it in range(ITERS):
        row_all(it).wait_send()
    for k in range(3):
        mass_copy(k).wait_send()
        fin_copy(k).wait_send()


def on_device(passages, centroids):
    lists = centroids.shape[0]
    chunks = OWN // CHUNK
    dma = pltpu.SemaphoreType.DMA
    vm = pltpu.VMEM
    new, mass = pl.pallas_call(
        body,
        out_shape=(
            jax.ShapeDtypeStruct((WIDTH, lists), F32),
            jax.ShapeDtypeStruct((2, 128), F32),
        ),
        in_specs=[pl.BlockSpec(memory_space=pl.ANY)] * 2,
        out_specs=(pl.BlockSpec(memory_space=pltpu.VMEM),) * 2,
        scratch_shapes=[
            vm((OWN, D), BF16),
            vm((MINE, D), BF16),
            vm((ROWS, D), BF16),
            vm((ROWS, D), BF16),
            vm((LISTS, D), BF16),
            vm((LISTS, ROWS), F32),
            vm((LISTS, ROWS), BF16),
            vm((LISTS, 128), F32),
            vm((LISTS, 128), F32),
            vm((ITERS + 2, LT, 128), F32),
            vm((ITERS + 1, len(PEERS), LT, 128), F32),
            vm((ITERS, RT, 128), F32),
            vm((ITERS, 7, RT, 128), F32),
            vm((2, 3, GROUP, D), BF16),
            vm((2, 2, GROUP, D), BF16),
            vm((2, 2, GROUP // 2, D), BF16),
            vm((2, 2, GROUP // 2, D), F32),
            vm((2, GROUP, D), F32),
            vm((2, 3, SUB, D), BF16),
            vm((2, 3, SUB, D), BF16),
            vm((4, MINE, WIDTH), BF16),
            vm((4, MINE, WIDTH), BF16),
            vm((128, 128), F32),
            vm((MINE, 128), F32),
            vm((4, 8, 128), F32),
            dma((2,)),
            dma((2, 3)), dma((2, 3)),
            dma((2, 4, 2, 3)), dma((2, 4, 2, 3)),
            dma((chunks,)), dma((chunks,)),
            dma((2, chunks)), dma((2, chunks)),
            dma((chunks,)), dma((chunks,)),
            dma((3, chunks)), dma((3, chunks)),
            dma((ITERS + 1,)), dma((ITERS + 1,)),
            dma((ITERS,)), dma((ITERS,)),
            dma((2, 2, 2, 3)), dma((2, 2, 2, 3)),
            dma((2, 2, 3)), dma((2, 2, 3)),
            dma((3,)), dma((3,)),
            dma((3,)), dma((3,)),
        ],
        compiler_params=pltpu.CompilerParams(
            collective_id=0, has_side_effects=True, vmem_limit_bytes=60 * 1024 * 1024
        ),
        cost_estimate=pl.CostEstimate(
            flops=4 * LISTS * ROWS * D, bytes_accessed=2 * 1024 * 1024, transcendentals=LISTS * ROWS
        ),
        name="sinkhorn",
    )(passages, centroids)
    return new.T, mass.reshape(lists)


def solution(mesh):
    return jax.shard_map(
        on_device,
        mesh=mesh,
        in_specs=(P(("dp", "list"), None), P("list", None)),
        out_specs=(P("list", "dp"), P("list")),
        check_vma=False,
    )
```

time: 106 us -> 101 us (0.953)
  Pallas kernels: 103 us -> 98.2 us
    pallas_call x1, Pallas kernels: 103 us -> 98.2 us  [on_device(): pl.pallas_call(body, out_shape=(jax.ShapeDtypeStruct((WIDTH, lists), F32)...]
where the time goes in v4:
time: 101 us
  Pallas kernels  98.2 us (97%)
  local copies, waits for them, and re-layouts  2.18 us (2%)
    pallas_call x1, Pallas kernels, on_device(): pl.pallas_call(body, out_shape=(jax.ShapeDtypeStruct((WIDTH, lists), F32)...  98.2 us
    unnamed x4, local copies, waits for them, and re-layouts  2.18 us

profile of v4, /device:TPU:1, one launch (start us, length us, event | category | flops | bytes accessed | tf_op | source)
XLA Modules:
  0.0 101.1 jit_solution(8617972043788228643)
XLA Ops:
  0.6 98.2 %sinkhorn.1 = (f32[192,256]{1,0:T(8,128)}, f32[2,128]{1,0:T(2,128)}) custom-call(bf16[512,768]{1,0:T(8,128)(2,1)} %p_hbm.1, bf16[256,768]{1,0:T(8,128)(2,1)} %cent_hbm.1), custom_call_target="tpu_custom_call" | custom-call | flops 12884901888 | bytes 2097152 | tf_op jit(solution)/shard_map/sinkhorn/pallas_call | solution.py:528
  98.9 0.0 copy-start
  98.9 1.6 %copy.6 = f32[256,192]{0,1:T(8,128)} copy(f32[256,192]{0,1:T(8,128)} %bitcast.2) | data formatting | bytes 393216
  100.5 0.0 copy-done
  100.5 0.6 copy.7
Async XLA Ops:
  98.9 1.6 %copy-start = (f32[2,128]{1,0:T(2,128)S(1)}, f32[2,128]{1,0:T(2,128)}, u32[]{:S(2)}) copy-start(f32[2,128]{1,0:T(2,128)} %get-tuple-element.5) | copy-start | bytes 3076

commit v5 on v4

--- a/solution.py
+++ b/solution.py
@@ -21,6 +21,7 @@
 MINE = 2 * SUB
 LT = LISTS // 128
 RT = ROWS // 128
+HT = RT // 2
 TARGET = 8.0
 LOG2E20 = 20.0 * 1.4426950408889634
 
@@ -46,10 +47,11 @@
 
 
 def body(
-    p_hbm, cent_hbm, out_ref, mass_ref,
-    P_in, C_in, U, Us, C, K, Kb, csum, cb, colbuf, colrecv, rowbuf, rowrecv,
+    p_hbm, cent_hbm, out_hbm, mass_hbm,
+    out_ref, mass_ref,
+    P_in, C_in, U, C, K, csum, cb, colbuf, colrecv, rowbuf, rowrecv,
     Sb, Sr, Rl, Acc, Own, Tb, Tr, Fs, Fr, wt, wbuf, mbuf,
-    in_s, a0_s, a0_r, a1_s, a1_r, ps_s, ps_r, pz_s, pz_r, pr_s, pr_r, pf_s, pf_r, col_s, col_r, row_s, row_r,
+    in_s, out_s, a0_s, a0_r, a1_s, a1_r, ps_s, ps_r, pz_s, pz_r, pr_s, pr_r, pf_s, pf_r, col_s, col_r, row_s, row_r,
     rs_s, rs_r, r2_s, r2_r, fin_s, fin_r, m_s, m_r,
 ):
     dp = lax.axis_index("dp")
@@ -156,13 +158,11 @@
     def p_fwd(d, k, sent=True):
         return p_copy(d, c if sent else 1 - c, k, pf_s.at[d - 1, k], pf_r.at[d - 1, k], sibling)
 
-    def p_near(k):
-        for way in (0, 1):
-            p_z(k, way, False).wait_recv()
-            if (k < 2) == (way == 0):
-                p_relay(k).start()
-        for d in (1, 3):
-            p_fwd(d, k).start()
+    def p_near(way, k):
+        p_z(k, way, False).wait_recv()
+        if (k < 2) == (way == 0):
+            p_relay(k).start()
+        p_fwd(3 if way == 0 else 1, k).start()
 
     def p_far(k):
         p_relay(k, False).wait_recv()
@@ -178,9 +178,8 @@
         C[pl.ds(at, SUB), :] = unit(C_in[pl.ds(h * SUB, SUB), :])
 
     pl.semaphore_wait(barrier, len(peers))
-    for k in (0, 2):
-        for way in (0, 1):
-            p_z(k, way).start()
+    for way in (0, 1):
+        p_z(2 * way, way).start()
     for h in (0, 1):
         for d in (1, 3):
             a0_copy(h, d).start()
@@ -189,9 +188,9 @@
     a1_start(0, 0)
     for k in range(chunks):
         p_sib(k).start()
-    for k in (1, 3):
+    for k in (1, 2, 3):
         for way in (0, 1):
-            p_z(k, way).start()
+            p_z((k + 2 * way) % 4, way).start()
 
     def gemm1(at, m, qt, n, first):
         s = lax.dot_general(
@@ -200,7 +199,6 @@
         )
         e = jnp.exp2(s * LOG2E20)
         K[pl.ds(at, m), pl.ds(qt, n)] = e
-        Kb[pl.ds(at, m), pl.ds(qt, n)] = e.astype(BF16)
         part = [e[:, t * 128 : (t + 1) * 128] for t in range(n // 128)]
         while len(part) > 1:
             part = [part[t] + part[t + 1] for t in range(0, len(part), 2)]
@@ -209,10 +207,9 @@
     def group_at(h, step):
         return pl.multiple_of(h * HALFLISTS + (place(h, 1)[0] + step) % 4 * GROUP, GROUP)
 
-    def own_gemm(steps):
-        for step in steps:
-            for h in (0, 1):
-                gemm1(group_at(h, step), GROUP, pl.multiple_of(z * 1024, 1024), 1024, True)
+    def own_gemm():
+        for g in range(0, LISTS, 256):
+            gemm1(g, 256, pl.multiple_of(z * 1024, 1024), 1024, True)
 
     def far_gemm(d, k):
         at = pl.multiple_of((z + d) % 4 * 1024 + k * 256, 256)
@@ -235,60 +232,60 @@
     a1_relay(0)
     for k in range(chunks):
         p_sib(k, False).wait_recv()
-    own_gemm((0,))
+    p_near(0, 0)
+    p_near(1, 2)
     a1_relay(1)
     a1_relay(3)
-    p_near(0)
     a1_relay(2)
-    for j in (0, 1, 3, 2):
-        a1_wait(j, 1)
-    own_gemm((1, 3))
-    p_near(2)
-    for j in (0, 1, 3, 2):
-        a1_wait(j, 2)
-    own_gemm((2,))
-    p_near(1)
-
-    def far_both(k):
-        for d in (1, 3):
-            p_fwd(d, k, False).wait_recv()
-        for d in (1, 3):
-            far_gemm(d, k)
-
-    def far_two(k):
-        p_fwd(2, k, False).wait_recv()
-        far_gemm(2, k)
-
-    far_both(0)
+    p_near(0, 1)
+    p_near(1, 3)
+    for k in (1, 2):
+        for j in (0, 1, 3, 2):
+            a1_wait(j, k)
+    own_gemm()
+
+    def far(d, k):
+        p_fwd(d, k, False).wait_recv()
+        far_gemm(d, k)
+
+    p_near(0, 2)
+    p_near(1, 0)
+    far(3, 0)
+    far(1, 2)
+    far(3, 1)
+    far(1, 3)
+    p_near(0, 3)
+    p_near(1, 1)
+    far(3, 2)
+    far(1, 0)
     p_far(0)
-    far_both(2)
-    p_near(3)
     p_far(2)
-    far_both(1)
-    far_two(0)
+    far(3, 3)
+    far(1, 1)
+    far(2, 0)
+    far(2, 2)
     p_far(1)
-    far_two(2)
-    far_both(3)
     p_far(3)
-    far_two(1)
-    far_two(3)
-
-    def col_pass(r16, out):
+    far(2, 1)
+    far(2, 3)
+
+    def col_pass(half, r16):
         strips = 32
 
         @pl.loop(0, LISTS // (8 * strips))
         def _(i):
             acc = [None] * strips
-            for t in range(RT):
+            for t in range(HT):
                 r = jnp.broadcast_to(r16[t : t + 1, :], (8, 128))
+                lanes = slice((half * HT + t) * 128, (half * HT + t + 1) * 128)
                 for s in range(strips):
                     at = pl.multiple_of(i * (8 * strips) + s * 8, 8)
-                    term = K[pl.ds(at, 8), t * 128 : (t + 1) * 128] * r
+                    term = K[pl.ds(at, 8), lanes] * r
+                    if t == 0 and half == 1:
+                        term += csum[pl.ds(at, 8), :]
                     acc[s] = term if acc[s] is None else acc[s] + term
             for s in range(strips):
                 csum[pl.ds(pl.multiple_of(i * (8 * strips) + s * 8, 8), 8), :] = acc[s]
-
-        fold(out)
 
     def fold(out):
         parts = []
@@ -308,69 +305,73 @@
         col_all(it).wait_recv()
         return jnp.sum(colrecv[it], axis=0) + colbuf[it]
 
-    def row_pass(c16):
-        for b in range(LT):
-            cb[b * 128 : (b + 1) * 128, :] = spread(c16[b : b + 1, :])
-
+    def row_pass(half):
         def step(i, acc):
             acc = list(acc)
             for s in range(8):
                 at = pl.multiple_of(i * 64 + s * 8, 8)
                 scale = cb[pl.ds(at, 8), :]
-                for t in range(RT):
-                    acc[t] += K[pl.ds(at, 8), t * 128 : (t + 1) * 128] * scale
+                for t in range(HT):
+                    acc[t] += K[pl.ds(at, 8), (half * HT + t) * 128 : (half * HT + t + 1) * 128] * scale
             return tuple(acc)
 
-        zero = tuple(jnp.zeros((8, 128), F32) for _ in range(RT))
+        zero = tuple(jnp.zeros((8, 128), F32) for _ in range(HT))
         acc = lax.fori_loop(0, LISTS // 64, step, zero)
         return jnp.concatenate([jnp.sum(a, axis=0, keepdims=True) for a in acc], axis=0)
 
     row_peers = [up(2, 1 - c), up(2, c)] + [up(d, 1 - c) for d in (1, 3)] + [up(d, c) for d in (1, 3)] + [sibling]
 
-    def row_send(it, value):
-        rowbuf[it] = value
+    def row_send(it, half, value):
+        rowbuf[it, half] = value
         for k, peer in enumerate(row_peers):
-            remote(rowbuf.at[it], rowrecv.at[it, k], row_s.at[it], row_r.at[it], peer).start()
-
-    def row_all(it):
-        return remote(rowrecv.at[it], rowrecv.at[it], row_s.at[it], row_r.at[it], sibling)
-
-    def row_sum(it, value):
-        row_send(it, value)
-        row_all(it).wait_recv()
-        return jnp.sum(rowrecv[it], axis=0) + value
-
-    r16 = None
+            remote(
+                rowbuf.at[it, half], rowrecv.at[it, half, k], row_s.at[it, half], row_r.at[it, half], peer
+            ).start()
+
+    def row_all(it, half):
+        got = rowrecv.at[it, half]
+        return remote(got, got, row_s.at[it, half], row_r.at[it, half], sibling)
+
+    def row_take(it, half):
+        row_all(it, half).wait_recv()
+        return 1.0 / (jnp.sum(rowrecv[it, half], axis=0) + rowbuf[it, half])
+
     for it in range(ITERS):
-        if it == 0:
-            fold(colbuf.at[0])
-        else:
-            col_pass(r16, colbuf.at[it])
+        if it > 0:
+            for half in (0, 1):
+                col_pass(half, row_take(it - 1, half))
+        fold(colbuf.at[it])
         col_send(it)
-        r16 = 1.0 / row_sum(it, row_pass(TARGET / col_take(it)))
-
-    def scale_rows(first, count):
-        for b in range(first, first + count):
-            scale = spread(r16[b : b + 1, :])
-            wide = U[b * 128 : (b + 1) * 128, :].astype(F32)
-            Us[b * 128 : (b + 1) * 128, :] = (
-                wide * jnp.concatenate([scale] * (D // 128), axis=1)
-            ).astype(BF16)
-
-    def gemm2(h, step):
-        return jnp.dot(Kb[pl.ds(group_at(h, step), GROUP), :], Us[...], preferred_element_type=F32)
-
-    def gemm2_first(h, step, parts=8):
-        total = None
+        c16 = TARGET / col_take(it)
+        for b in range(LT):
+            cb[b * 128 : (b + 1) * 128, :] = spread(c16[b : b + 1, :])
+        for half in (0, 1):
+            row_send(it, half, row_pass(half))
+
+    last = {}
+
+    def gemm2(groups, parts=4):
         n = ROWS // parts
+        total, mass = None, [None] * len(groups)
         for q in range(parts):
-            scale_rows(q * (RT // parts), RT // parts)
-            part = jnp.dot(
-                Kb[pl.ds(group_at(h, step), GROUP), q * n : (q + 1) * n], Us[q * n : (q + 1) * n, :],
-                preferred_element_type=F32,
-            )
-            total = part if total is None else total + part
-        return total
+            half = q * 2 // parts
+            if half not in last:
+                last[half] = row_take(ITERS - 1, half)
+            first = q * n // 128 - half * HT
+            scale = jnp.concatenate([last[half][t : t + 1, :] for t in range(first, first + n // 128)], axis=1)
+            plans = []
+            for i, (h, step) in enumerate(groups):
+                plan = K[pl.ds(group_at(h, step), GROUP), q * n : (q + 1) * n] * scale
+                part = [plan[:, t * 128 : (t + 1) * 128] for t in range(n // 128)]
+                while len(part) > 1:
+                    part = [part[t] + part[t + 1] for t in range(0, len(part), 2)]
+                mass[i] = part[0] if mass[i] is None else mass[i] + part[0]
+                plans.append(plan.astype(BF16))
+            soft = jnp.dot(jnp.concatenate(plans, axis=0), U[q * n : (q + 1) * n, :], preferred_element_type=F32)
+            total = soft if total is None else total + soft
+        for i, (h, step) in enumerate(groups):
+            csum[pl.ds(group_at(h, step), GROUP), :] = mass[i]
+        return [total[i * GROUP : (i + 1) * GROUP, :] for i in range(len(groups))]
 
     HALF = GROUP // 2
 
@@ -394,30 +395,50 @@
         Sb[h, way, half, cols(w)] = (Acc[h, way, :, cols(w)] + Rl[h, way, :, cols(w)].astype(F32)).astype(BF16)
         rs_copy(h, w, way, 2).start()
 
-    for h in (0, 1):
-        Sb[h, 2] = (gemm2_first if h == 0 else gemm2)(h, 2).astype(BF16)
-        for w in (0, 1):
+    for h, value in enumerate(gemm2([(0, 2), (1, 2)])):
+        Sb[h, 2] = value.astype(BF16)
+    for w in (0, 1):
+        for h in (0, 1):
             for way in (0, 1):
                 rs_copy(h, w, way, 0).start()
 
-    for way, step in ((0, 1), (1, 3)):
-        for h in (0, 1):
-            value = gemm2(h, step)
-            other = 1 - way
-            Sb[h, way, pl.ds(other * HALF, HALF), :] = value[other * HALF : (other + 1) * HALF, :].astype(BF16)
-            Acc[h, way] = value[way * HALF : (way + 1) * HALF, :]
-            rs_copy(h, 0, way, 1).start()
     for way in (0, 1):
-        for h in (0, 1):
-            rs_add(h, 0, way)
-            rs_copy(h, 1, way, 1).start()
-    for h in (0, 1):
-        Own[h] = gemm2(h, 0)
-    for way in (0, 1):
-        for h in (0, 1):
-            rs_add(h, 1, way)
-    col_pass(r16, colbuf.at[ITERS])
+        values = gemm2([(h, 1 if way == 0 else 3) for h in (0, 1)])
+        other = 1 - way
+        for h in (0, 1):
+            Sb[h, way, pl.ds(other * HALF, HALF), :] = values[h][other * HALF : (other + 1) * HALF, :].astype(BF16)
+            Acc[h, way] = values[h][way * HALF : (way + 1) * HALF, :]
+        for w in (0, 1):
+            for h in (0, 1):
+                rs_copy(h, w, way, 1).start()
+    for h, value in enumerate(gemm2([(0, 0), (1, 0)])):
+        Own[h] = value
+    for w in (0, 1):
+        for way in (0, 1):
+            for h in (0, 1):
+                rs_add(h, w, way)
+    fold(colbuf.at[ITERS])
     col_send(ITERS)
+
+    def r2_copy(h, w, d):
+        lanes = pl.ds(w * WAVE, WAVE)
+        return remote(
+            Tb.at[h, d - 1, :, lanes], Tr.at[h, d - 1, :, lanes],
+            r2_s.at[h, w, d - 1], r2_r.at[h, w, d - 1], along(h, 0, d),
+        )
+
+    def sub(h, d):
+        return pl.ds(pl.multiple_of((place(h, 0)[0] + d) % 4 * SUB, SUB), SUB)
+
+    for w in (0, 1):
+        for h in (0, 1):
+            for way in (0, 1):
+                for k in (1, 2):
+                    rs_copy(h, w, way, k).wait_recv()
+            Own[h, :, cols(w)] += Sr[h, 0, :, cols(w)].astype(F32) + Sr[h, 1, :, cols(w)].astype(F32)
+            for d in (2, 1, 3):
+                Tb[h, d - 1, :, cols(w)] = Own[h, sub(h, d), cols(w)].astype(BF16)
+                r2_copy(h, w, d).start()
 
     colbuf[ITERS + 1] = col_take(ITERS)
     held = []
@@ -442,26 +463,6 @@
     for k in range(3):
         mass_copy(k).start()
 
-    def r2_copy(h, w, d):
-        lanes = pl.ds(w * WAVE, WAVE)
-        return remote(
-            Tb.at[h, d - 1, :, lanes], Tr.at[h, d - 1, :, lanes],
-            r2_s.at[h, w, d - 1], r2_r.at[h, w, d - 1], along(h, 0, d),
-        )
-
-    def sub(h, d):
-        return pl.ds(pl.multiple_of((place(h, 0)[0] + d) % 4 * SUB, SUB), SUB)
-
-    for w in (0, 1):
-        for h in (0, 1):
-            for way in (0, 1):
-                for k in (1, 2):
-                    rs_copy(h, w, way, k).wait_recv()
-            Own[h, :, cols(w)] += Sr[h, 0, :, cols(w)].astype(F32) + Sr[h, 1, :, cols(w)].astype(F32)
-            for d in (2, 1, 3):
-                Tb[h, d - 1, :, cols(w)] = Own[h, sub(h, d), cols(w)].astype(BF16)
-                r2_copy(h, w, d).start()
-
     def fin_copy(k, sent=True):
         to = fin_peers[k][1]
         return remote(Fs.at[to if sent else dp], Fr.at[dp if sent else to], fin_s.at[k], fin_r.at[k], fin_peers[k][0])
@@ -484,6 +485,8 @@
     for k in (0, 1):
         mass_ref[k : k + 1, :] = jnp.concatenate([mbuf[2 * k, 0:1, 0:MINE], mbuf[2 * k + 1, 0:1, 0:MINE]], axis=1)
 
+    mass_out = pltpu.make_async_copy(mass_ref, mass_hbm, out_s.at[1])
+    mass_out.start()
     Fr[dp] = Fs[dp]
     for k in (2, 1, 0):
         fin_copy(k, False).wait_recv()
@@ -492,6 +495,9 @@
         out_ref[0:128, k * 128 : (k + 1) * 128] = value[:, 0:128].T
         side = jnp.concatenate([value[:, 128:192], jnp.zeros((128, 64), F32)], axis=1)
         out_ref[128:192, k * 128 : (k + 1) * 128] = side.T[0:64, :]
+
+    new_out = pltpu.make_async_copy(out_ref, out_hbm, out_s.at[0])
+    new_out.start()
 
     for h in (0, 1):
         for d in (1, 2, 3):
@@ -514,10 +520,13 @@
     for it in range(ITERS + 1):
         col_all(it).wait_send()
     for it in range(ITERS):
-        row_all(it).wait_send()
+        for half in (0, 1):
+            row_all(it, half).wait_send()
     for k in range(3):
         mass_copy(k).wait_send()
         fin_copy(k).wait_send()
+    mass_out.wait()
+    new_out.wait()
 
 
 def on_device(passages, centroids):
@@ -532,21 +541,21 @@
             jax.ShapeDtypeStruct((2, 128), F32),
         ),
         in_specs=[pl.BlockSpec(memory_space=pl.ANY)] * 2,
-        out_specs=(pl.BlockSpec(memory_space=pltpu.VMEM),) * 2,
+        out_specs=(pl.BlockSpec(memory_space=pl.ANY),) * 2,
         scratch_shapes=[
+            vm((WIDTH, lists), F32),
+            vm((2, 128), F32),
             vm((OWN, D), BF16),
             vm((MINE, D), BF16),
             vm((ROWS, D), BF16),
-            vm((ROWS, D), BF16),
             vm((LISTS, D), BF16),
             vm((LISTS, ROWS), F32),
-            vm((LISTS, ROWS), BF16),
             vm((LISTS, 128), F32),
             vm((LISTS, 128), F32),
             vm((ITERS + 2, LT, 128), F32),
             vm((ITERS + 1, len(PEERS), LT, 128), F32),
-            vm((ITERS, RT, 128), F32),
-            vm((ITERS, 7, RT, 128), F32),
+            vm((ITERS, 2, HT, 128), F32),
+            vm((ITERS, 2, 7, HT, 128), F32),
             vm((2, 3, GROUP, D), BF16),
             vm((2, 2, GROUP, D), BF16),
             vm((2, 2, GROUP // 2, D), BF16),
@@ -560,6 +569,7 @@
             vm((MINE, 128), F32),
             vm((4, 8, 128), F32),
             dma((2,)),
+            dma((2,)),
             dma((2, 3)), dma((2, 3)),
             dma((2, 4, 2, 3)), dma((2, 4, 2, 3)),
             dma((chunks,)), dma((chunks,)),
@@ -567,7 +577,7 @@
             dma((chunks,)), dma((chunks,)),
             dma((3, chunks)), dma((3, chunks)),
             dma((ITERS + 1,)), dma((ITERS + 1,)),
-            dma((ITERS,)), dma((ITERS,)),
+            dma((ITERS, 2)), dma((ITERS, 2)),
             dma((2, 2, 2, 3)), dma((2, 2, 2, 3)),
             dma((2, 2, 3)), dma((2, 2, 3)),
             dma((3,)), dma((3,)),

time: 101 us -> 96.7 us (0.957)
  Pallas kernels: 98.2 us -> 93.8 us
    pallas_call x1, Pallas kernels: 98.2 us -> 93.8 us  [on_device(): pl.pallas_call(body, out_shape=(jax.ShapeDtypeStruct((WIDTH, lists), F32)...]
where the time goes in v5:
time: 96.7 us; the launch traced here: 96.6 us
  Pallas kernels  93.8 us (97%)
  local copies, waits for them, and re-layouts  2.18 us (2%)
    pallas_call x1, Pallas kernels, on_device(): pl.pallas_call(body, out_shape=(jax.ShapeDtypeStruct((WIDTH, lists), F32)...  93.8 us
    unnamed x4, local copies, waits for them, and re-layouts  2.18 us

profile of v5, /device:TPU:1, one launch (start us, length us, event | category | flops | bytes accessed | tf_op | source)
XLA Modules:
  0.0 96.6 jit_solution(3106924556189056291)
XLA Ops:
  0.6 93.8 %sinkhorn.1 = (f32[192,256]{1,0:T(8,128)}, f32[2,128]{1,0:T(2,128)}) custom-call(bf16[512,768]{1,0:T(8,128)(2,1)} %p_hbm.1, bf16[256,768]{1,0:T(8,128)(2,1)} %cent_hbm.1), custom_call_target="tpu_custom_call" | custom-call | flops 12884901888 | bytes 2097152 | tf_op jit(solution)/shard_map/sinkhorn/pallas_call | solution.py:537
  94.4 0.0 copy-start
  94.4 1.6 %copy.6 = f32[256,192]{0,1:T(8,128)} copy(f32[256,192]{0,1:T(8,128)} %bitcast.2) | data formatting | bytes 393216
  96.0 0.0 copy-done
  96.0 0.6 copy.7
Async XLA Ops:
  94.4 1.6 %copy-start = (f32[2,128]{1,0:T(2,128)S(1)}, f32[2,128]{1,0:T(2,128)}, u32[]{:S(2)}) copy-start(f32[2,128]{1,0:T(2,128)} %get-tuple-element.5) | copy-start | bytes 3076

commit v6 on v5

--- a/solution.py
+++ b/solution.py
@@ -540,7 +540,7 @@
             jax.ShapeDtypeStruct((WIDTH, lists), F32),
             jax.ShapeDtypeStruct((2, 128), F32),
         ),
-        in_specs=[pl.BlockSpec(memory_space=pl.ANY)] * 2,
+        in_specs=[pl.BlockSpec(memory_space=pltpu.HBM)] * 2,
         out_specs=(pl.BlockSpec(memory_space=pl.ANY),) * 2,
         scratch_shapes=[
             vm((WIDTH, lists), F32),
@@ -584,7 +584,7 @@
             dma((3,)), dma((3,)),
         ],
         compiler_params=pltpu.CompilerParams(
-            collective_id=0, has_side_effects=True, vmem_limit_bytes=60 * 1024 * 1024
+            collective_id=0, has_side_effects=True, vmem_limit_bytes=48 * 1024 * 1024
         ),
         cost_estimate=pl.CostEstimate(
             flops=4 * LISTS * ROWS * D, bytes_accessed=2 * 1024 * 1024, transcendentals=LISTS * ROWS

time: 96.7 us -> 97.5 us (level)
  local copies, waits for them, and re-layouts: 2.18 us -> 3.36 us
    unnamed x4 -> x6, local copies, waits for them, and re-layouts: 2.18 us -> 3.36 us
where the time goes in v6:
time: 97.5 us; the launch traced here: 97.3 us
  Pallas kernels  93.3 us (96%)
  local copies, waits for them, and re-layouts  3.36 us (3%)
    pallas_call x1, Pallas kernels, on_device(): pl.pallas_call(body, out_shape=(jax.ShapeDtypeStruct((WIDTH, lists), F32)...  93.3 us
    unnamed x6, local copies, waits for them, and re-layouts  3.36 us

profile of v6, /device:TPU:1, one launch (start us, length us, event | category | flops | bytes accessed | tf_op | source)
XLA Modules:
  0.0 97.3 jit_solution(16140777484320129100)
XLA Ops:
  0.6 0.0 copy-start
  0.6 1.1 %copy-done = bf16[512,768]{1,0:T(8,128)(2,1)S(1)} copy-done((bf16[512,768]{1,0:T(8,128)(2,1)S(1)}, bf16[512,768]{1,0:T(8,128)(2,1)}, u32[]{:S(2)}) %copy-start) | copy-done | bytes 786456
  1.8 0.0 copy-start.1
  1.8 1.0 %copy-done.1 = bf16[256,768]{1,0:T(8,128)(2,1)S(1)} copy-done((bf16[256,768]{1,0:T(8,128)(2,1)S(1)}, bf16[256,768]{1,0:T(8,128)(2,1)}, u32[]{:S(2)}) %copy-start.1) | copy-done | bytes 393240
  2.8 93.3 %sinkhorn.1 = (f32[192,256]{1,0:T(8,128)S(1)}, f32[2,128]{1,0:T(2,128)S(1)}) custom-call(bf16[512,768]{1,0:T(8,128)(2,1)S(1)} %copy-done, bf16[256,768]{1,0:T(8,128)(2,1)S(1)} %copy-done.1), custom_call_target="tpu_custom_call" | custom-call | flops 12884901888 | bytes 2097152 | tf_op jit(solution)/shard_map/sinkhorn/pallas_call | solution.py:537
  96.0 0.7 copy.6
  96.7 0.6 copy.7
Async XLA Ops:
  0.6 1.1 %copy-start = (bf16[512,768]{1,0:T(8,128)(2,1)S(1)}, bf16[512,768]{1,0:T(8,128)(2,1)}, u32[]{:S(2)}) copy-start(bf16[512,768]{1,0:T(8,128)(2,1)} %p_hbm.1) | copy-start | bytes 2359300
  1.8 1.0 %copy-start.1 = (bf16[256,768]{1,0:T(8,128)(2,1)S(1)}, bf16[256,768]{1,0:T(8,128)(2,1)}, u32[]{:S(2)}) copy-start(bf16[256,768]{1,0:T(8,128)(2,1)} %cent_hbm.1) | copy-start | bytes 1179652

commit v7 on v5

--- a/solution.py
+++ b/solution.py
@@ -244,30 +244,26 @@
             a1_wait(j, k)
     own_gemm()
 
-    def far(d, k):
-        p_fwd(d, k, False).wait_recv()
-        far_gemm(d, k)
+    def far(*pairs):
+        for d, k in pairs:
+            p_fwd(d, k, False).wait_recv()
+        for d, k in pairs:
+            far_gemm(d, k)
 
     p_near(0, 2)
     p_near(1, 0)
-    far(3, 0)
-    far(1, 2)
-    far(3, 1)
-    far(1, 3)
+    far((3, 0), (1, 2))
+    far((3, 1), (1, 3))
     p_near(0, 3)
     p_near(1, 1)
-    far(3, 2)
-    far(1, 0)
+    far((3, 2), (1, 0))
     p_far(0)
     p_far(2)
-    far(3, 3)
-    far(1, 1)
-    far(2, 0)
-    far(2, 2)
+    far((3, 3), (1, 1))
+    far((2, 0), (2, 2))
     p_far(1)
     p_far(3)
-    far(2, 1)
-    far(2, 3)
+    far((2, 1), (2, 3))
 
     def col_pass(half, r16):
         strips = 32

time: 96.7 us -> 96.9 us (level)
  no operation moved by 1% of the time
where the time goes in v7:
time: 96.9 us; the launch traced here: 96.8 us
  Pallas kernels  93.9 us (97%)
  local copies, waits for them, and re-layouts  2.18 us (2%)
    pallas_call x1, Pallas kernels, on_device(): pl.pallas_call(body, out_shape=(jax.ShapeDtypeStruct((WIDTH, lists), F32)...  93.9 us
    unnamed x4, local copies, waits for them, and re-layouts  2.18 us

profile of v7, /device:TPU:1, one launch (start us, length us, event | category | flops | bytes accessed | tf_op | source)
XLA Modules:
  0.0 96.8 jit_solution(15681752407486607883)
XLA Ops:
  0.6 93.9 %sinkhorn.1 = (f32[192,256]{1,0:T(8,128)}, f32[2,128]{1,0:T(2,128)}) custom-call(bf16[512,768]{1,0:T(8,128)(2,1)} %p_hbm.1, bf16[256,768]{1,0:T(8,128)(2,1)} %cent_hbm.1), custom_call_target="tpu_custom_call" | custom-call | flops 12884901888 | bytes 2097152 | tf_op jit(solution)/shard_map/sinkhorn/pallas_call | solution.py:533
  94.6 0.0 copy-start
  94.6 1.6 %copy.6 = f32[256,192]{0,1:T(8,128)} copy(f32[256,192]{0,1:T(8,128)} %bitcast.2) | data formatting | bytes 393216
  96.2 0.0 copy-done
  96.2 0.6 copy.7
Async XLA Ops:
  94.6 1.6 %copy-start = (f32[2,128]{1,0:T(2,128)S(1)}, f32[2,128]{1,0:T(2,128)}, u32[]{:S(2)}) copy-start(f32[2,128]{1,0:T(2,128)} %get-tuple-element.5) | copy-start | bytes 3076
